TPU v7x, 768 devices: a whole 4x8x12 slice. The times are simulated.
768 devices in a mesh: layer: 4 (over y_lo), gx: 24 (over z, core), gy: 8 (over x, y_hi).
Axes of the slice: x: 4, y: 8 (y_hi: 2, y_lo: 4; y = y_hi * 4 + y_lo), z: 12, core: 2. Of those that a mesh axis runs over, the one named last changes fastest.
Arguments:
- wave: bfloat16 [13, 4, 24, 6, 6, 6, 1024], P(None, 'layer', 'gx', None, None, None, 'gy'), may hold values from -36 to 36
- adjoint_source: bfloat16 [13, 4, 24, 6, 6, 6, 1024], P(None, 'layer', 'gx', None, None, None, 'gy'), may hold values from -36 to 36
- coupling: float32 [4, 3, 13, 13], P('layer'), may hold values from -1 to 1
- stiffness: float32 [13, 4, 24, 1024], P(None, 'layer', 'gx', 'gy'), may hold values from 0.5 to 2
- partner: int32 [4, 24, 1024], P(None, 'gx', 'gy'), may hold values from 0 to 3, as said below
- owner: int32 [4, 24, 1024], P('layer', 'gx', 'gy'), may hold values from 0 to 1023
Outputs:
- final_wave: bfloat16 [13, 4, 24, 6, 6, 6, 1024], P(None, 'layer', 'gx', None, None, None, 'gy')
- adjoint_wave: bfloat16 [13, 4, 24, 6, 6, 6, 1024], P(None, 'layer', 'gx', None, None, None, 'gy')
- cell_kernel: float32 [4, 24, 13, 1024], P('layer', 'gx', None, 'gy')
Inputs may be any that keep to these rules, and one draw needn't show every extreme that they name: `partner`: in every element column each depth group is named exactly once.
All inputs are finite; a program needn't handle non-finite values.
Results may differ from a plain program's by a relative error of at most 0.005.
Values may be sent and summed in bfloat16 or wider, within the bound.
No kernel may reach another device: no remote copies, remote signals or barrier semaphores. Data moves between devices by JAX's collectives and lax.ppermute only.
A program may use at most 128 MiB of HBM per device.

v0:
```python
import functools
import math

import jax
import jax.numpy as jnp
import numpy as np
from jax import lax
from jax.experimental import pallas as pl
from jax.experimental.pallas import tpu as pltpu
from jax.sharding import PartitionSpec as P

F = 13
ROWS = 16
NP = 6
EY = 128
CELLS_DEV = 128
BOTTOM = 4
HALF = 64
S_RIGHT = 36
S_LEFT = 100
DT = 0.05
TAU = 7.5
F32 = jnp.float32
BF16 = jnp.bfloat16
VMEM_LIMIT = 40 * 1024 * 1024


def lobatto_derivative():
    outer = math.sqrt(1.0 / 3.0 + 2.0 * math.sqrt(7.0) / 21.0)
    inner = math.sqrt(1.0 / 3.0 - 2.0 * math.sqrt(7.0) / 21.0)
    nodes = np.array([-1.0, -outer, -inner, inner, outer, 1.0])
    weights = np.array(
        [
            1.0 / np.prod([nodes[col] - nodes[other] for other in range(6) if other != col])
            for col in range(6)
        ]
    )
    table = np.zeros((6, 6))
    for row_id in range(6):
        for col in range(6):
            if row_id != col:
                table[row_id, col] = weights[col] / weights[row_id] / (nodes[row_id] - nodes[col])
        table[row_id, row_id] = -np.sum(table[row_id])
    return table


def lane_ids(rows):
    return lax.broadcasted_iota(jnp.int32, (rows, EY), 1)


def load_scale(stiff_ref, scale):
    for f in range(F):
        scale[f : f + 1, :] = stiff_ref[f]
    return scale[0:F, :]


def prep_kernel(
    wave_ref, adj_ref, stiff_ref, second_ref, first_ref, bottom_ref,
    raw, kept, low, stiff, scale, rows, trace, sems,
):
    odd = lax.rem(lax.axis_index("gx"), 2)
    near = 5 * (1 - odd)
    far = 5 * odd
    copies = []

    def send(src, dst):
        copies.append(pltpu.make_async_copy(src, dst, sems.at[len(copies)]))
        copies[-1].start()
        return copies[-1]

    arrivals = [
        send(stiff_ref, stiff),
        send(adj_ref.at[:, :, 0], low.at[1]),
        send(wave_ref.at[:, :, 0], low.at[0]),
        send(adj_ref.at[far], raw.at[1]),
        send(adj_ref.at[near], raw.at[0]),
    ]
    arrivals += [send(wave_ref.at[far], kept.at[1]), send(wave_ref.at[near], kept.at[0])]
    leaving = []
    for copy in arrivals[0:3]:
        copy.wait()
    s = load_scale(stiff, scale)
    s4 = s[0:BOTTOM]
    for part in range(2):
        for a in range(NP):
            for b in range(NP):
                x = low[part, a, b].astype(F32)[0:BOTTOM]
                if part == 1:
                    x = x * s4
                k = BOTTOM * (a * NP + b)
                rows[k : k + BOTTOM, :] = x
        trace[part] = rows[...].astype(BF16)
    for group in range(bottom_ref.shape[0]):
        leaving.append(send(trace, bottom_ref.at[group]))
    for out_ref, at in ((second_ref, 1), (first_ref, 0)):
        arrivals[6 - at].wait()
        leaving.append(send(kept.at[at], out_ref.at[0]))
    for out_ref, at in ((second_ref, 1), (first_ref, 0)):
        arrivals[4 - at].wait()
        for b in range(NP):
            for c in range(NP):
                raw[at, b, c] = (raw[at, b, c].astype(F32) * s).astype(BF16)
        leaving.append(send(raw.at[at], out_ref.at[1]))
    for copy in leaving:
        copy.wait()


def build_matrices(side, coup_ref, cs, mats):
    table = lobatto_derivative()
    cs[...] = jnp.zeros_like(cs)
    for d in range(3):
        for f in range(F):
            cs[d, f : f + 1, 0:F] = coup_ref[d, f]
    block = lane_ids(ROWS) // ROWS
    spread = []
    for i in range(NP):
        row = jnp.zeros((ROWS, EY), F32)
        for k in range(NP):
            row = jnp.where(block == k, F32(table[i, k]), row)
        spread.append(row)
    for d in range(3):
        base = cs[d]
        if side == 1:
            base = -jnp.concatenate([base, jnp.zeros((EY - ROWS, EY), F32)], axis=0).T[0:ROWS]
        wide = base
        for k in range(1, NP):
            wide = wide + pltpu.roll(base, ROWS * k, 1)
        for i in range(NP):
            mats[d, ROWS * i : ROWS * (i + 1), :] = (wide * spread[i]).astype(BF16)


def put(edge, tile, frm, to):
    return jnp.where(lane_ids(F) == to, pltpu.roll(tile, (to - frm) % EY, 1), edge)


def inner_kernel(
    wave_ref, adj_ref, stiff_ref, coup_ref,
    new_wave_ref, new_adj_ref, side_out_ref, top_out_ref, strip_out_ref, small_out_ref,
    scale, cs, mats, padded, packed, acc, mid, side_ref, top_ref, strip_ref, small, coup, sems,
):
    copies = []

    def send(src, dst):
        copies.append(pltpu.make_async_copy(src, dst, sems.at[len(copies)]))
        copies[-1].start()
        return copies[-1]

    arrival = send(coup_ref, coup)
    s = load_scale(stiff_ref, scale)
    for a in range(NP):
        padded[:, a, :, :, 8:ROWS, :] = jnp.zeros((2, NP, NP, ROWS - 8, EY), F32)
        for b in range(NP):
            for c in range(NP):
                padded[0, a, b, c, 0:F, :] = wave_ref[a, b, c].astype(F32)
                padded[1, a, b, c, 0:F, :] = adj_ref[a, b, c].astype(F32) * s
        for side in range(2):
            packed[side, a] = padded[side, a].astype(BF16)
    arrival.wait()
    small[0, 0:F, :] = s

    def leave(side, a):
        out_ref = new_adj_ref if side else new_wave_ref
        if a in (0, 5):
            send(side_ref.at[side, a // 5], side_out_ref.at[side, a // 5])
        else:
            send(mid.at[side, a - 1], out_ref.at[a, 1:5, 0:5])
            send(top_ref.at[side, a - 1], top_out_ref.at[side, a - 1])
            send(strip_ref.at[side, a - 1], strip_out_ref.at[side, a - 1])

    for side in range(2):
        inner_side(
            side, adj_ref, s, coup, side_ref, top_ref, strip_ref, small,
            cs, mats, padded.at[side], packed.at[side], acc, mid, leave,
        )
    send(small, small_out_ref)
    for copy in copies[1:]:
        copy.wait()


def inner_side(
    side, adj_ref, s, coup_ref, side_ref, top_ref, strip_ref, small,
    cs, mats, padded, packed, acc, mid, leave,
):
    width = NP * ROWS
    lanes = lane_ids(F)
    row_ids = lax.broadcasted_iota(jnp.int32, (F, EY), 0)

    build_matrices(side, coup_ref, cs, mats)
    m = [mats[d][:, 0:width] for d in range(3)]
    for b in range(NP):
        right = jnp.concatenate([packed[:, b, c].reshape(width, EY) for c in range(NP)], axis=1)
        out = jnp.dot(m[0], right, preferred_element_type=F32)
        for c in range(NP):
            acc[:, b, c] = out[:, c * EY : (c + 1) * EY].reshape(NP, ROWS, EY)

    total = jnp.zeros((F, EY), F32)
    u_edge = jnp.zeros((F, EY), F32)
    lam_edge = jnp.zeros((F, EY), F32)
    edge = jnp.zeros((F, EY), F32)
    for a in range(NP):
        right = jnp.concatenate([packed[a, :, c].reshape(width, EY) for c in range(NP)], axis=1)
        along_b = jnp.dot(m[1], right, preferred_element_type=F32)
        right = jnp.concatenate([packed[a, b].reshape(width, EY) for b in range(NP)], axis=1)
        along_c = jnp.dot(m[2], right, preferred_element_type=F32)
        for b in range(NP):
            for c in range(NP):
                rate = (
                    acc[a, b, c]
                    + along_b[ROWS * b : ROWS * (b + 1), c * EY : (c + 1) * EY]
                    + along_c[ROWS * c : ROWS * (c + 1), b * EY : (b + 1) * EY]
                )[0:F]
                v = padded[a, b, c, 0:F, :]
                face = None
                own = (a in (0, 5)) + (b in (0, 5))
                if b == 0:
                    other = padded[a, 5, c, 0:F, :]
                    face = jnp.where(lanes == 0, 0.0, pltpu.roll(other, 1, 1))
                if b == 5:
                    other = padded[a, 0, c, 0:F, :]
                    face = jnp.where(lanes == EY - 1, 0.0, pltpu.roll(other, EY - 1, 1))
                if own:
                    rate = rate - (TAU * own) * v
                if face is not None:
                    rate = rate + TAU * face
                if c == 5:
                    rate = rate - jnp.where(row_ids < BOTTOM, TAU * v, 0.0)
                k = a * NP + c
                lam = adj_ref[a, b, c].astype(F32)
                if side == 0:
                    total = total + lam * rate
                    new = v + (DT * s) * rate
                else:
                    new = lam + DT * rate
                if a in (0, 5):
                    side_ref[side, a // 5, b, c] = rate.astype(BF16)
                elif c == 5:
                    top_ref[side, a - 1, b] = rate.astype(BF16)
                elif b in (0, 5):
                    strip_ref[side, a - 1, b // 5, c] = new.astype(BF16)
                else:
                    mid[side, a - 1, b - 1, c] = new.astype(BF16)
                if b == 0 and a not in (0, 5) and c != 5:
                    edge = put(edge, new, 0, HALF * (1 - side) + k)
                if b == 5 and a not in (0, 5) and c != 5:
                    edge = put(edge, new, EY - 1, HALF * side + k)
                if side == 0 and b == 0:
                    u_edge = put(u_edge, v, 0, k)
                    lam_edge = put(lam_edge, lam, 0, HALF + k)
                if side == 0 and b == 5:
                    u_edge = put(u_edge, v, EY - 1, HALF + k)
                    lam_edge = put(lam_edge, lam, EY - 1, k)
        leave(side, a)
    small[1 + side, 0:F, :] = edge
    if side == 0:
        small[3, 0:F, :] = total
        left = jnp.sum(jnp.where(lanes == 0, s, 0.0), axis=1, keepdims=True)
        right = jnp.sum(jnp.where(lanes == EY - 1, s, 0.0), axis=1, keepdims=True)
        lam_edge = jnp.where(lanes == S_RIGHT, right, jnp.where(lanes == S_LEFT, left, lam_edge))
        small[4, 0:F, :] = u_edge
        small[5, 0:F, :] = lam_edge
        small[6, 0:F, :] = jnp.where(lanes < HALF, right, left)


def load_floors(side, mate, bottom_ref, floors):
    pick = bottom_ref[0, side].astype(F32)
    for group in range(1, bottom_ref.shape[0]):
        pick = jnp.where(mate == group, bottom_ref[group, side].astype(F32), pick)
    for k in range(NP * NP):
        floors[k, 0:BOTTOM, :] = pick[BOTTOM * k : BOTTOM * (k + 1)]


def outside(side, a, b, c, odd, first_ref, second_ref, floors):
    face = None
    if a in (0, 5):
        one, two = first_ref[side, b, c], second_ref[side, b, c]
        near = jnp.where(odd, one, two) if a == 0 else jnp.where(odd, two, one)
        face = near.astype(F32)
    if c == 5:
        row_ids = lax.broadcasted_iota(jnp.int32, (F, EY), 0)
        x = jnp.where(row_ids < BOTTOM, floors[a * NP + b], 0.0)
        face = x if face is None else face + x
    return face


def outer_kernel(
    first_ref, second_ref, bottom_ref, adj_ref, partner_hbm, owner_hbm, small_hbm,
    send_ref, mate_ref,
    floors, tile, partner_ref, owner_ref, small, sems,
):
    arrivals = [
        pltpu.make_async_copy(src, dst, sems.at[i])
        for i, (src, dst) in enumerate(
            ((small_hbm, small), (partner_hbm, partner_ref), (owner_hbm, owner_ref))
        )
    ]
    for copy in arrivals:
        copy.start()
    odd = lax.rem(lax.axis_index("gx"), 2) == 1
    total = jnp.zeros((F, EY), F32)
    for a in (0, 5):
        for b in range(NP):
            for c in range(5):
                face = outside(0, a, b, c, odd, first_ref, second_ref, floors)
                total = total + adj_ref[a, b, c].astype(F32) * face
    for copy in arrivals:
        copy.wait()
    mate = partner_ref[lax.axis_index("layer")]
    mate_ref[...] = mate
    load_floors(0, mate, bottom_ref, floors)
    for a in range(NP):
        for b in range(NP):
            face = outside(0, a, b, 5, odd, first_ref, second_ref, floors)
            total = total + adj_ref[a, b, 5].astype(F32) * face
    total = small[3, 0:F, :] + TAU * total
    total = DT * total
    high = total.astype(BF16)
    rest = total - high.astype(F32)
    middle = rest.astype(BF16)
    low = (rest - middle.astype(F32)).astype(BF16)
    owner = owner_ref[0]
    count = send_ref.shape[0]
    lane = lane_ids(1)
    own_left = jnp.sum(jnp.where(lane == 0, owner, 0), axis=1, keepdims=True).astype(F32)
    own_right = jnp.sum(jnp.where(lane == EY - 1, owner, 0), axis=1, keepdims=True).astype(F32)
    zeros = jnp.zeros((1, EY), F32)
    tile[...] = jnp.zeros_like(tile)
    for i in range(2):
        tile[0:F, :] = small[4 + i, 0:F, :]
        end = tile[...].astype(BF16)
        for target in range(count):
            send_ref[target, (2 + i) * ROWS : (3 + i) * ROWS, :] = end
    tile[F : F + 1, :] = zeros + own_left
    tile[F + 1 : F + 2, :] = zeros + own_right
    for target in range(count):
        cells = lax.broadcasted_iota(jnp.int32, (CELLS_DEV, EY), 0) + CELLS_DEV * target
        held = (cells == owner).astype(BF16)
        tile[0:F, :] = sum(
            lax.dot_general(x, held, (((1,), (1,)), ((), ())), preferred_element_type=F32)
            for x in (low, middle, high)
        )
        whole = tile[...]
        top = whole.astype(BF16)
        send_ref[target, 0:ROWS, :] = top
        send_ref[target, ROWS : 2 * ROWS, :] = (whole - top.astype(F32)).astype(BF16)


def last_kernel(
    got_ref, small, strip_ref, side_ref, top_ref, second_ref, first_ref, bottom_ref, mate_ref,
    wave_ref, adj_ref, old_wave_ref, old_adj_ref,
    new_wave_ref, new_adj_ref, cell_ref,
    patched, side_new, top_new, cell, floors, sems,
):
    me = lax.axis_index("gy")
    odd = lax.rem(lax.axis_index("gx"), 2) == 1
    mate = mate_ref[...]
    count = got_ref.shape[0]
    copies = []

    def send(src, dst):
        copies.append(pltpu.make_async_copy(src, dst, sems.at[len(copies)]))
        copies[-1].start()

    s = small[0, 0:F, :]
    factors = DT * s, DT

    def finished(side, a, b, c):
        rate = (side_ref[side, a // 5, b, c] if a in (0, 5) else top_ref[side, a - 1, b]).astype(F32)
        rate = rate + TAU * outside(side, a, b, c, odd, first_ref, second_ref, floors.at[side])
        return (adj_ref if side else wave_ref)[a, b, c].astype(F32) + factors[side] * rate

    for side, out_ref in ((0, new_wave_ref), (1, new_adj_ref)):
        load_floors(side, mate, bottom_ref, floors.at[side])
        for a in range(NP):
            for b in range(1, 5):
                if a in (0, 5):
                    for c in range(NP):
                        side_new[side, a // 5, b - 1, c] = finished(side, a, b, c).astype(BF16)
                else:
                    top_new[side, a - 1, b - 1] = finished(side, a, b, 5).astype(BF16)
            if a in (0, 5):
                send(side_new.at[side, a // 5], out_ref.at[a, 1:5])
        send(top_new.at[side], out_ref.at[1:5, 1:5, 5])
    lanes = lane_ids(F)
    upper = lanes >= HALF

    def tile(j, i):
        return got_ref[j, ROWS * i : ROWS * (i + 1), :].astype(F32)

    cells = jnp.zeros((F, EY), F32)
    lane = (lane_ids(1) + CELLS_DEV * me).astype(F32)
    for j in range(count):
        sums = tile(j, 0) + tile(j, 1)
        cells = cells + sums[0:F]
        lam = tile(j, 3)[0:F]
        for other, side, row in ((j - 1, upper, F), (j + 1, lanes < HALF, F + 1)):
            if 0 <= other < count:
                pairs = jnp.where(side, lam * tile(other, 2)[0:F], 0.0)
                value = (DT * TAU) * jnp.sum(pairs, axis=1, keepdims=True)
                cells = cells + jnp.where(sums[row : row + 1] == lane, value, 0.0)
    for f in range(F):
        cell[f] = cells[f : f + 1]
    send(cell, cell_ref)

    below = lax.max(me - 1, 0)
    above = lax.min(me + 1, count - 1)

    def held(values, column):
        return jnp.sum(jnp.where(lanes == column, values, 0.0), axis=1, keepdims=True)

    for side, out_ref in ((0, new_wave_ref), (1, new_adj_ref)):
        low = jnp.where(me > 0, tile(below, 2 + side)[0:F], 0.0)
        high = jnp.where(me < count - 1, tile(above, 2 + side)[0:F], 0.0)
        if side == 0:
            near = jnp.where(upper, low, high) * small[6, 0:F, :]
        else:
            near = jnp.where(upper, high * held(high, S_LEFT), low * held(low, S_RIGHT))
        near = (DT * TAU) * near
        edge = small[1 + side, 0:F, :] + near
        for b, end, start in ((0, 0, HALF if side == 0 else 0), (1, EY - 1, 0 if side == 0 else HALF)):
            for a in range(NP):
                for c in range(NP):
                    shift = (end - start - a * NP - c) % EY
                    if a in (0, 5) or c == 5:
                        old = finished(side, a, 5 * b, c)
                        moved = old + pltpu.roll(near, shift, 1)
                    else:
                        old = strip_ref[side, a - 1, b, c].astype(F32)
                        moved = pltpu.roll(edge, shift, 1)
                    patched[side, b, a, c] = jnp.where(lanes == end, moved, old).astype(BF16)
            send(patched.at[side, b], out_ref.at[:, 5 * b])
    for copy in copies:
        copy.wait()


def swap(x, axis, pairs):
    return lax.ppermute(x, axis, [(i, j) for i, j in pairs] + [(j, i) for i, j in pairs])


def per_device(wave, adjoint_source, coupling, stiffness, partner, owner):
    wave = wave[:, 0, 0].transpose(1, 2, 3, 0, 4)
    adj = adjoint_source[:, 0, 0].transpose(1, 2, 3, 0, 4)
    stiff = stiffness[:, 0]
    coup = coupling[0][:, :, None, :]
    own = owner[0]
    layers, columns, count = (lax.axis_size(axis) for axis in ("layer", "gx", "gy"))
    field = jax.ShapeDtypeStruct((NP, NP, NP, F, EY), BF16)
    faces = jax.ShapeDtypeStruct((2, NP, NP, F, EY), BF16)
    traces = jax.ShapeDtypeStruct((layers, 2, BOTTOM * NP * NP, EY), BF16)
    vmem = pl.BlockSpec(memory_space=pltpu.VMEM)
    hbm = pl.BlockSpec(memory_space=pltpu.HBM)
    params = pltpu.CompilerParams(vmem_limit_bytes=VMEM_LIMIT)

    def far(*arrays):
        return tuple(pltpu.with_memory_space_constraint(x, pltpu.HBM) for x in arrays)

    second, first, bottom = pl.pallas_call(
        prep_kernel,
        out_shape=(faces, faces, traces),
        in_specs=[hbm] * 3,
        out_specs=(hbm,) * 3,
        scratch_shapes=[
            pltpu.VMEM((2, NP, NP, F, EY), BF16),
            pltpu.VMEM((2, NP, NP, F, EY), BF16),
            pltpu.VMEM((2, NP, NP, F, EY), BF16),
            pltpu.VMEM((F, 1, EY), F32),
            pltpu.VMEM((ROWS, EY), F32),
            pltpu.VMEM((BOTTOM * NP * NP, EY), F32),
            pltpu.VMEM(traces.shape[1:], BF16),
            pltpu.SemaphoreType.DMA((11 + layers,)),
        ],
        compiler_params=params,
    )(*far(wave, adj, stiff))

    second = swap(second, "gx", [(i, i + 1) for i in range(1, columns - 1, 2)])
    first = swap(first, "gx", [(i, i + 1) for i in range(0, columns - 1, 2)])
    bottom = lax.all_to_all(bottom, "layer", 0, 0, tiled=True)

    side_shape, top_shape, strip_shape = (2, 2, NP, NP, F, EY), (2, 4, NP, F, EY), (2, 4, 2, 5, F, EY)
    small_shape = (7, ROWS, EY)
    new_wave, new_adj, sides, tops, strips, small = pl.pallas_call(
        inner_kernel,
        out_shape=(
            pltpu.HBM(field.shape, BF16),
            pltpu.HBM(field.shape, BF16),
            pltpu.HBM(side_shape, BF16),
            pltpu.HBM(top_shape, BF16),
            pltpu.HBM(strip_shape, BF16),
            pltpu.HBM(small_shape, F32),
        ),
        in_specs=[vmem] * 3 + [hbm],
        out_specs=(hbm,) * 6,
        scratch_shapes=[
            pltpu.VMEM((ROWS, EY), F32),
            pltpu.VMEM((3, ROWS, EY), F32),
            pltpu.VMEM((3, NP * ROWS, EY), BF16),
            pltpu.VMEM((2, NP, NP, NP, ROWS, EY), F32),
            pltpu.VMEM((2, NP, NP, NP, ROWS, EY), BF16),
            pltpu.VMEM((NP, NP, NP, ROWS, EY), F32),
            pltpu.VMEM((2, 4, 4, 5, F, EY), BF16),
            pltpu.VMEM(side_shape, BF16),
            pltpu.VMEM(top_shape, BF16),
            pltpu.VMEM(strip_shape, BF16),
            pltpu.VMEM(small_shape, F32),
            pltpu.VMEM(coup.shape, F32),
            pltpu.SemaphoreType.DMA((30,)),
        ],
        compiler_params=params,
        cost_estimate=pl.CostEstimate(flops=2**31, bytes_accessed=2**23, transcendentals=0),
    )(wave, adj, stiff, *far(coup))

    send, mate = pl.pallas_call(
        outer_kernel,
        out_shape=(
            jax.ShapeDtypeStruct((count, 4 * ROWS, EY), BF16),
            jax.ShapeDtypeStruct((1, EY), jnp.int32),
        ),
        in_specs=[vmem] * 4 + [hbm] * 3,
        out_specs=(vmem,) * 2,
        scratch_shapes=[
            pltpu.VMEM((NP * NP, F, EY), F32),
            pltpu.VMEM((ROWS, EY), F32),
            pltpu.VMEM(partner.shape, jnp.int32),
            pltpu.VMEM(own.shape, jnp.int32),
            pltpu.VMEM(small_shape, F32),
            pltpu.SemaphoreType.DMA((3,)),
        ],
        compiler_params=params,
    )(first, second, bottom, adj, *far(partner, own, small))

    got = lax.all_to_all(send, "gy", 0, 0, tiled=True)

    new_wave, new_adj, cells = pl.pallas_call(
        last_kernel,
        out_shape=(field, field, jax.ShapeDtypeStruct((F, 1, CELLS_DEV), F32)),
        in_specs=[vmem] * 11 + [hbm] * 2,
        out_specs=(hbm,) * 3,
        scratch_shapes=[
            pltpu.VMEM((2, 2, NP, NP, F, EY), BF16),
            pltpu.VMEM((2, 2, 4, NP, F, EY), BF16),
            pltpu.VMEM((2, 4, 4, F, EY), BF16),
            pltpu.VMEM((F, 1, CELLS_DEV), F32),
            pltpu.VMEM((2, NP * NP, F, EY), F32),
            pltpu.SemaphoreType.DMA((11,)),
        ],
        input_output_aliases={11: 0, 12: 1},
        compiler_params=params,
    )(got, small, strips, sides, tops, second, first, bottom, mate, wave, adj, new_wave, new_adj)

    new_wave = new_wave.transpose(3, 0, 1, 2, 4)[:, None, None]
    new_adj = new_adj.transpose(3, 0, 1, 2, 4)[:, None, None]
    return (new_wave, new_adj, cells.transpose(1, 0, 2)[None])


def solution(mesh):
    return jax.shard_map(
        per_device,
        mesh=mesh,
        in_specs=(
            P(None, "layer", "gx", None, None, None, "gy"),
            P(None, "layer", "gx", None, None, None, "gy"),
            P("layer", None, None, None),
            P(None, "layer", "gx", "gy"),
            P(None, "gx", "gy"),
            P("layer", "gx", "gy"),
        ),
        out_specs=(
            P(None, "layer", "gx", None, None, None, "gy"),
            P(None, "layer", "gx", None, None, None, "gy"),
            P("layer", "gx", None, "gy"),
        ),
        check_vma=False,
    )
```

profile of v0, /device:TPU:1, one launch (start us, length us, event | category | flops | bytes accessed | tf_op | source)
XLA Modules:
  0.0 42.1 jit_solution(5340599526887103089)
XLA Ops:
  0.6 0.0 copy-start
  0.6 0.0 copy-start.1
  0.6 2.3 %shard_map.85 = (bf16[2,6,6,13,128]{4,3,2,1,0:T(8,128)(2,1)S(1)}, bf16[2,6,6,13,128]{4,3,2,1,0:T(8,128)(2,1)S(1)}, bf16[4,2,144,128]{3,2,1,0:T(8,128)(2,1)}) custom-call(bf16[6,6,6,13,128]{4,3,2,1,0:T(8,128)(2,1)} %bitcast.22, bf16[6,6,6,13,128]{4,3,2,1,0:T(8,128)(2,1)} %bitcast.18, f32[13,1,128]{2,1,0:T(1,128)} %bitcast.25), custom_call_target="tpu_custom_call" | custom-call | tf_op jit(solution)/shard_map/pallas_call | solution.py:456
  2.9 0.0 copy-start.6
  3.0 5.4 %all-to-all-start = ((bf16[4,2,144,128]{3,2,1,0:T(8,128)(2,1)}), bf16[4,2,144,128]{3,2,1,0:T(8,128)(2,1)S(1)}, u32[]{:S(2)}, u32[]{:S(2)}) async-start(bf16[4,2,144,128]{3,2,1,0:T(8,128)(2,1)} %get-tuple-element.19), calls=%async_computation | async-start | bytes 589824 | tf_op jit(solution)/shard_map/all_to_all | solution.py:476
  8.4 10.5 %collective-permute-start = (bf16[2,6,6,13,128]{4,3,2,1,0:T(8,128)(2,1)S(1)}, bf16[2,6,6,13,128]{4,3,2,1,0:T(8,128)(2,1)S(1)}, u32[]{:S(2)}, u32[]{:S(2)}) collective-permute-start(bf16[2,6,6,13,128]{4,3,2,1,0:T(8,128)(2,1)S(1)} %get-tuple-element.17), channel_id=1, source_target_pairs={{0,8},{16,24},{32,40},{48,56},{64,72},{80,88},{96,104},{112,120},{... | collective-permute-start | bytes 718856 | tf_op jit(solution)/shard_map/ppermute | solution.py:436
  18.9 1.9 %collective-permute-start.1 = (bf16[2,6,6,13,128]{4,3,2,1,0:T(8,128)(2,1)S(1)}, bf16[2,6,6,13,128]{4,3,2,1,0:T(8,128)(2,1)S(1)}, u32[]{:S(2)}, u32[]{:S(2)}) collective-permute-start(bf16[2,6,6,13,128]{4,3,2,1,0:T(8,128)(2,1)S(1)} %get-tuple-element.18), channel_id=1, source_target_pairs={{8,16},{24,32},{40,48},{56,64},{72,80},{88,96},{104,112},{120,128}... | collective-permute-start | bytes 718856 | tf_op jit(solution)/shard_map/ppermute | solution.py:436
  20.8 0.0 copy-done
  20.8 0.0 copy-done.1
  20.8 0.0 copy-done.6
  20.8 3.8 %shard_map.86 = (bf16[6,6,6,13,128]{4,3,2,1,0:T(8,128)(2,1)}, bf16[6,6,6,13,128]{4,3,2,1,0:T(8,128)(2,1)}, bf16[2,2,6,6,13,128]{5,4,3,2,1,0:T(8,128)(2,1)}, bf16...) custom-call(bf16[6,6,6,13,128]{4,3,2,1,0:T(8,128)(2,1)S(1)} %bitcast.23, ...), custom_call_target="tpu_custom_call" | custom-call | flops 2147483648 | bytes 8388608 | tf_op jit(solution)/shard_map/pallas_call | solution.py:480
  24.6 0.0 collective-permute-done.first_ref
  24.6 2.3 %collective-permute-done.1.second_ref = bf16[2,6,6,13,128]{4,3,2,1,0:T(8,128)(2,1)S(1)} collective-permute-done((bf16[2,6,6,13,128]{4,3,2,1,0:T(8,128)(2,1)S(1)}, bf16[2,6,6,13,128]{4,3,2,1,0:T(8,128)(2,1)S(1)}, u32[]{:S(2)}, u32[]{:S(2)}) %collective-permute-start.1) | collective-permute-done | bytes 239648 | tf_op jit(solution)/shard_map/ppermute | solution.py:436
  26.9 0.0 all-to-all-done.bottom_ref
  26.9 0.0 copy-start.2
  26.9 0.0 copy-start.3
  26.9 1.5 %shard_map.87 = (bf16[8,64,128]{2,1,0:T(8,128)(2,1)S(1)}, s32[1,128]{1,0:T(1,128)S(1)}) custom-call(bf16[2,6,6,13,128]{4,3,2,1,0:T(8,128)(2,1)S(1)} %collective-permute-done.first_ref, bf16[2,6,6,13,128]{4,3,2,1,0:T(8,128)(2,1)S(1)} %collective-permute-done.1.second_ref, bf16[4,2,144,128]{3,2,1,0:T(8,128)(2,1)S(1)} %all-to-all-done.bottom_ref, ...), custom_call_target="tpu_custom_call" | custom-call | tf_op jit(solution)/shard_map/pallas_call | solution.py:511
  28.4 0.0 copy-start.5
  28.5 0.0 copy-start.4
  28.5 12.0 %all_to_all.10.got_ref = bf16[8,64,128]{2,1,0:T(8,128)(2,1)S(1)} all-to-all(bf16[8,64,128]{2,1,0:T(8,128)(2,1)S(1)} %get-tuple-element.21), channel_id=1, replica_groups=mesh['layer'=4,'gx'=24,'gy'=8] {'gy'}, dimensions={0} | all-to-all | bytes 262144 | tf_op jit(solution)/shard_map/all_to_all | solution.py:530
  40.4 0.0 copy-done.2
  40.4 0.0 copy-done.3
  40.4 0.0 copy-done.5
  40.4 0.0 copy-done.4
  40.5 1.6 %shard_map.88 = (bf16[6,6,6,13,128]{4,3,2,1,0:T(8,128)(2,1)}, bf16[6,6,6,13,128]{4,3,2,1,0:T(8,128)(2,1)}, f32[13,1,128]{2,1,0:T(1,128)}) custom-call(bf16[8,64,128]{2,1,0:T(8,128)(2,1)S(1)} %all_to_all.10.got_ref, f32[7,16,128]{2,1,0:T(8,128)S(1)} %copy-done.4, ...), custom_call_target="tpu_custom_call", output_to_operand_aliasing={{0}: (11, {}), {1}: (12, {})} | custom-call | tf_op jit(solution)/shard_map/pallas_call | solution.py:532
Async XLA Ops:
  0.6 20.2 %copy-start = (bf16[13,1,1,6,6,6,128]{6,0,5,4,3,2,1:T(8,128)(2,1)S(1)}, bf16[13,1,1,6,6,6,128]{6,0,5,4,3,2,1:T(8,128)(2,1)}, u32[]{:S(2)}) copy-start(bf16[13,1,1,6,6,6,128]{6,0,5,4,3,2,1:T(8,128)(2,1)} %param.7) | copy-start | bytes 2156548
  0.6 20.2 %copy-start.1 = (bf16[13,1,1,6,6,6,128]{6,0,5,4,3,2,1:T(8,128)(2,1)S(1)}, bf16[13,1,1,6,6,6,128]{6,0,5,4,3,2,1:T(8,128)(2,1)}, u32[]{:S(2)}) copy-start(bf16[13,1,1,6,6,6,128]{6,0,5,4,3,2,1:T(8,128)(2,1)} %param.6) | copy-start | bytes 2156548
  2.9 17.9 %copy-start.6 = (f32[13,1,1,128]{3,2,1,0:T(1,128)S(1)}, f32[13,1,1,128]{3,2,1,0:T(1,128)}, u32[]{:S(2)}) copy-start(f32[13,1,1,128]{3,2,1,0:T(1,128)} %param.9) | copy-start | bytes 19972
  3.0 23.9 %all-to-all-start = ((bf16[4,2,144,128]{3,2,1,0:T(8,128)(2,1)}), bf16[4,2,144,128]{3,2,1,0:T(8,128)(2,1)S(1)}, u32[]{:S(2)}, u32[]{:S(2)}) async-start(bf16[4,2,144,128]{3,2,1,0:T(8,128)(2,1)} %get-tuple-element.19), calls=%async_computation | async-start | bytes 589824 | tf_op jit(solution)/shard_map/all_to_all | solution.py:476
  8.4 16.3 %collective-permute-start = (bf16[2,6,6,13,128]{4,3,2,1,0:T(8,128)(2,1)S(1)}, bf16[2,6,6,13,128]{4,3,2,1,0:T(8,128)(2,1)S(1)}, u32[]{:S(2)}, u32[]{:S(2)}) collective-permute-start(bf16[2,6,6,13,128]{4,3,2,1,0:T(8,128)(2,1)S(1)} %get-tuple-element.17), channel_id=1, source_target_pairs={{0,8},{16,24},{32,40},{48,56},{64,72},{80,88},{96,104},{112,120},{... | collective-permute-start | bytes 718856 | tf_op jit(solution)/shard_map/ppermute | solution.py:436
  18.9 8.0 %collective-permute-start.1 = (bf16[2,6,6,13,128]{4,3,2,1,0:T(8,128)(2,1)S(1)}, bf16[2,6,6,13,128]{4,3,2,1,0:T(8,128)(2,1)S(1)}, u32[]{:S(2)}, u32[]{:S(2)}) collective-permute-start(bf16[2,6,6,13,128]{4,3,2,1,0:T(8,128)(2,1)S(1)} %get-tuple-element.18), channel_id=1, source_target_pairs={{8,16},{24,32},{40,48},{56,64},{72,80},{88,96},{104,112},{120,128}... | collective-permute-start | bytes 718856 | tf_op jit(solution)/shard_map/ppermute | solution.py:436
  26.9 13.5 %copy-start.2 = (bf16[2,2,6,6,13,128]{5,4,3,2,1,0:T(8,128)(2,1)S(1)}, bf16[2,2,6,6,13,128]{5,4,3,2,1,0:T(8,128)(2,1)}, u32[]{:S(2)}) copy-start(bf16[2,2,6,6,13,128]{5,4,3,2,1,0:T(8,128)(2,1)} %get-tuple-element.23.side_ref) | copy-start | bytes 1437700
  26.9 13.5 %copy-start.3 = (bf16[2,4,2,5,13,128]{5,4,3,2,1,0:T(8,128)(2,1)S(1)}, bf16[2,4,2,5,13,128]{5,4,3,2,1,0:T(8,128)(2,1)}, u32[]{:S(2)}) copy-start(bf16[2,4,2,5,13,128]{5,4,3,2,1,0:T(8,128)(2,1)} %get-tuple-element.22.strip_ref) | copy-start | bytes 798724
  28.4 12.0 %copy-start.5 = (bf16[2,4,6,13,128]{4,3,2,1,0:T(8,128)(2,1)S(1)}, bf16[2,4,6,13,128]{4,3,2,1,0:T(8,128)(2,1)}, u32[]{:S(2)}) copy-start(bf16[2,4,6,13,128]{4,3,2,1,0:T(8,128)(2,1)} %get-tuple-element.24.top_ref) | copy-start | bytes 479236
  28.5 12.0 %copy-start.4 = (f32[7,16,128]{2,1,0:T(8,128)S(1)}, f32[7,16,128]{2,1,0:T(8,128)}, u32[]{:S(2)}) copy-start(f32[7,16,128]{2,1,0:T(8,128)} %get-tuple-element.20.small_hbm.small) | copy-start | bytes 172036
where the time goes:
time: 42.4 us; the launch traced here: 42.1 us
  starting transfers between devices  17.8 us (42%)
  blocking collectives  12 us (28%)
  Pallas kernels  9.22 us (22%)
  waiting for transfers between devices  2.26 us (5%)
  between operations  0.76 us (2%)
    ppermute x2, starting transfers between devices, swap(): lax.ppermute(x, axis, [(i, j) for i, j in pairs] + [(j, i) for i, j in pa...  12.4 us
    all_to_all x1, blocking collectives, per_device(): got = lax.all_to_all(send, 'gy', 0, 0, tiled=True)  12 us
    all_to_all x1, starting transfers between devices, per_device(): bottom = lax.all_to_all(bottom, 'layer', 0, 0, tiled=True)  5.43 us
    pallas_call x1, Pallas kernels, per_device(): pl.pallas_call(inner_kernel, out_shape=(pltpu.HBM(field.shape, BF16), plt...  3.81 us
    pallas_call x1, Pallas kernels, per_device(): pl.pallas_call(prep_kernel, out_shape=(faces, faces, traces), in_specs=[h...  2.28 us
    ppermute x2, waiting for transfers between devices, swap(): lax.ppermute(x, axis, [(i, j) for i, j in pairs] + [(j, i) for i, j in pa...  2.26 us
    pallas_call x1, Pallas kernels, per_device(): pl.pallas_call(last_kernel, out_shape=(field, field, jax.ShapeDtypeStruct...  1.6 us
    pallas_call x1, Pallas kernels, per_device(): pl.pallas_call(outer_kernel, out_shape=(jax.ShapeDtypeStruct((count, 4 *...  1.53 us
  transfers between devices with their start and end apart: 3, of which 1 were waited for; matrix products, arithmetic and copies ran while one was open for 0% of the time, Pallas kernels for 9%

commit v1 on v0

--- a/solution.py
+++ b/solution.py
@@ -282,36 +282,61 @@
     return face
 
 
-def outer_kernel(
-    first_ref, second_ref, bottom_ref, adj_ref, partner_hbm, owner_hbm, small_hbm,
-    send_ref, mate_ref,
-    floors, tile, partner_ref, owner_ref, small, sems,
+def trace_kernel(
+    bottom_ref, adj_hbm, partner_hbm, owner_hbm, small_hbm,
+    lam_side_ref, ends_ref, total_ref, owner_ref, mate_ref,
+    floors, partner_ref, small, lam_top, tile, sems,
 ):
-    arrivals = [
+    copies = [
         pltpu.make_async_copy(src, dst, sems.at[i])
         for i, (src, dst) in enumerate(
-            ((small_hbm, small), (partner_hbm, partner_ref), (owner_hbm, owner_ref))
+            (
+                (partner_hbm, partner_ref),
+                (adj_hbm.at[:, :, 5], lam_top),
+                (small_hbm, small),
+                (owner_hbm, owner_ref),
+                (adj_hbm.at[0], lam_side_ref.at[0]),
+                (adj_hbm.at[5], lam_side_ref.at[1]),
+            )
         )
     ]
-    for copy in arrivals:
+    for copy in copies:
         copy.start()
+    copies[0].wait()
+    mate = partner_ref[lax.axis_index("layer")]
+    mate_ref[...] = mate
+    floors[...] = jnp.zeros_like(floors)
+    load_floors(0, mate, bottom_ref, floors)
+    copies[1].wait()
+    total = jnp.zeros((F, EY), F32)
+    row_ids = lax.broadcasted_iota(jnp.int32, (F, EY), 0)
+    for a in range(NP):
+        for b in range(NP):
+            total = total + lam_top[a, b].astype(F32) * floors[a * NP + b]
+    copies[2].wait()
+    total_ref[...] = small[3, 0:F, :] + jnp.where(row_ids < BOTTOM, TAU * total, 0.0)
+    tile[...] = jnp.zeros_like(tile)
+    for i in range(2):
+        tile[0:F, :] = small[4 + i, 0:F, :]
+        ends_ref[i] = tile[...].astype(BF16)
+    for copy in copies[3:]:
+        copy.wait()
+
+
+def outer_kernel(
+    first_ref, second_ref, lam_side_ref, ends_ref, total_ref, owner_ref,
+    send_ref,
+    tile,
+):
     odd = lax.rem(lax.axis_index("gx"), 2) == 1
     total = jnp.zeros((F, EY), F32)
-    for a in (0, 5):
-        for b in range(NP):
-            for c in range(5):
-                face = outside(0, a, b, c, odd, first_ref, second_ref, floors)
-                total = total + adj_ref[a, b, c].astype(F32) * face
-    for copy in arrivals:
-        copy.wait()
-    mate = partner_ref[lax.axis_index("layer")]
-    mate_ref[...] = mate
-    load_floors(0, mate, bottom_ref, floors)
-    for a in range(NP):
-        for b in range(NP):
-            face = outside(0, a, b, 5, odd, first_ref, second_ref, floors)
-            total = total + adj_ref[a, b, 5].astype(F32) * face
-    total = small[3, 0:F, :] + TAU * total
+    for b in range(NP):
+        for c in range(NP):
+            one, two = first_ref[0, b, c].astype(F32), second_ref[0, b, c].astype(F32)
+            low, high = jnp.where(odd, one, two), jnp.where(odd, two, one)
+            total = total + lam_side_ref[0, b, c].astype(F32) * low
+            total = total + lam_side_ref[1, b, c].astype(F32) * high
+    total = total_ref[...] + TAU * total
     total = DT * total
     high = total.astype(BF16)
     rest = total - high.astype(F32)
@@ -325,10 +350,8 @@
     zeros = jnp.zeros((1, EY), F32)
     tile[...] = jnp.zeros_like(tile)
     for i in range(2):
-        tile[0:F, :] = small[4 + i, 0:F, :]
-        end = tile[...].astype(BF16)
         for target in range(count):
-            send_ref[target, (2 + i) * ROWS : (3 + i) * ROWS, :] = end
+            send_ref[target, (2 + i) * ROWS : (3 + i) * ROWS, :] = ends_ref[i]
     tile[F : F + 1, :] = zeros + own_left
     tile[F + 1 : F + 2, :] = zeros + own_right
     for target in range(count):
@@ -508,24 +531,37 @@
         cost_estimate=pl.CostEstimate(flops=2**31, bytes_accessed=2**23, transcendentals=0),
     )(wave, adj, stiff, *far(coup))
 
-    send, mate = pl.pallas_call(
-        outer_kernel,
+    lam_sides, ends, total, own, mate = pl.pallas_call(
+        trace_kernel,
         out_shape=(
-            jax.ShapeDtypeStruct((count, 4 * ROWS, EY), BF16),
+            jax.ShapeDtypeStruct(side_shape[1:], BF16),
+            jax.ShapeDtypeStruct((2, ROWS, EY), BF16),
+            jax.ShapeDtypeStruct((F, EY), F32),
+            jax.ShapeDtypeStruct((1, EY), jnp.int32),
             jax.ShapeDtypeStruct((1, EY), jnp.int32),
         ),
-        in_specs=[vmem] * 4 + [hbm] * 3,
-        out_specs=(vmem,) * 2,
+        in_specs=[vmem] + [hbm] * 4,
+        out_specs=(vmem,) * 5,
         scratch_shapes=[
             pltpu.VMEM((NP * NP, F, EY), F32),
+            pltpu.VMEM(partner.shape, jnp.int32),
+            pltpu.VMEM(small_shape, F32),
+            pltpu.VMEM((NP, NP, F, EY), BF16),
             pltpu.VMEM((ROWS, EY), F32),
-            pltpu.VMEM(partner.shape, jnp.int32),
-            pltpu.VMEM(own.shape, jnp.int32),
-            pltpu.VMEM(small_shape, F32),
-            pltpu.SemaphoreType.DMA((3,)),
+            pltpu.SemaphoreType.DMA((6,)),
         ],
         compiler_params=params,
-    )(first, second, bottom, adj, *far(partner, own, small))
+        cost_estimate=pl.CostEstimate(flops=2**29, bytes_accessed=2**22, transcendentals=0),
+    )(bottom, *far(adj, partner, own, small))
+
+    send = pl.pallas_call(
+        outer_kernel,
+        out_shape=jax.ShapeDtypeStruct((count, 4 * ROWS, EY), BF16),
+        in_specs=[vmem] * 6,
+        out_specs=vmem,
+        scratch_shapes=[pltpu.VMEM((ROWS, EY), F32)],
+        compiler_params=params,
+    )(first, second, lam_sides, ends, total, own)
 
     got = lax.all_to_all(send, "gy", 0, 0, tiled=True)
 

time: 42.4 us -> 41.8 us (0.986)
  waiting for transfers between devices: 2.26 us -> 0.96 us
    ppermute x2, waiting for transfers between devices: 2.26 us -> 0.96 us  [swap(): lax.ppermute(x, axis, [(i, j) for i, j in pairs] + [(j, i) for i, j in pa...]
    pallas_call x1 -> x2, Pallas kernels: 1.53 us -> 1.85 us  [the longest x1 1.24 us: per_device(): pl.pallas_call(trace_kernel, out_shape=(jax.ShapeDtypeStruct(side_shape[1...]
  transfers between devices with their start and end apart: 3 -> 3, of which waited for: 1 -> 1; matrix products, arithmetic and copies ran while one was open for 0% -> 0% of each run, Pallas kernels for 9% -> 12%
where the time goes in v1:
time: 41.8 us; the launch traced here: 41.4 us
  starting transfers between devices  17.8 us (43%)
  blocking collectives  12.2 us (29%)
  Pallas kernels  9.56 us (23%)
  waiting for transfers between devices  0.96 us (2%)
  between operations  0.79 us (2%)
    ppermute x2, starting transfers between devices, swap(): lax.ppermute(x, axis, [(i, j) for i, j in pairs] + [(j, i) for i, j in pa...  12.4 us
    all_to_all x1, blocking collectives, per_device(): got = lax.all_to_all(send, 'gy', 0, 0, tiled=True)  12.2 us
    all_to_all x1, starting transfers between devices, per_device(): bottom = lax.all_to_all(bottom, 'layer', 0, 0, tiled=True)  5.43 us
    pallas_call x1, Pallas kernels, per_device(): pl.pallas_call(inner_kernel, out_shape=(pltpu.HBM(field.shape, BF16), plt...  3.82 us
    pallas_call x1, Pallas kernels, per_device(): pl.pallas_call(prep_kernel, out_shape=(faces, faces, traces), in_specs=[h...  2.28 us
    pallas_call x1, Pallas kernels, per_device(): pl.pallas_call(last_kernel, out_shape=(field, field, jax.ShapeDtypeStruct...  1.61 us
    pallas_call x1, Pallas kernels, per_device(): pl.pallas_call(trace_kernel, out_shape=(jax.ShapeDtypeStruct(side_shape[1...  1.24 us
    ppermute x2, waiting for transfers between devices, swap(): lax.ppermute(x, axis, [(i, j) for i, j in pairs] + [(j, i) for i, j in pa...  0.96 us
  transfers between devices with their start and end apart: 3, of which 1 were waited for; matrix products, arithmetic and copies ran while one was open for 0% of the time, Pallas kernels for 12%

profile of v1, /device:TPU:1, one launch (start us, length us, event | category | flops | bytes accessed | tf_op | source)
XLA Modules:
  0.0 41.4 jit_solution(3988272810832326444)
XLA Ops:
  0.6 0.0 copy-start
  0.6 0.0 copy-start.1
  0.7 2.3 %shard_map.85 = (bf16[2,6,6,13,128]{4,3,2,1,0:T(8,128)(2,1)S(1)}, bf16[2,6,6,13,128]{4,3,2,1,0:T(8,128)(2,1)S(1)}, bf16[4,2,144,128]{3,2,1,0:T(8,128)(2,1)}) custom-call(bf16[6,6,6,13,128]{4,3,2,1,0:T(8,128)(2,1)} %bitcast.18, bf16[6,6,6,13,128]{4,3,2,1,0:T(8,128)(2,1)} %bitcast.21, f32[13,1,128]{2,1,0:T(1,128)} %bitcast.25), custom_call_target="tpu_custom_call" | custom-call | tf_op jit(solution)/shard_map/pallas_call | solution.py:479
  2.9 0.0 copy-start.7
  3.0 5.4 %all-to-all-start = ((bf16[4,2,144,128]{3,2,1,0:T(8,128)(2,1)}), bf16[4,2,144,128]{3,2,1,0:T(8,128)(2,1)S(1)}, u32[]{:S(2)}, u32[]{:S(2)}) async-start(bf16[4,2,144,128]{3,2,1,0:T(8,128)(2,1)} %get-tuple-element.22), calls=%async_computation | async-start | bytes 589824 | tf_op jit(solution)/shard_map/all_to_all | solution.py:499
  8.4 10.5 %collective-permute-start = (bf16[2,6,6,13,128]{4,3,2,1,0:T(8,128)(2,1)S(1)}, bf16[2,6,6,13,128]{4,3,2,1,0:T(8,128)(2,1)S(1)}, u32[]{:S(2)}, u32[]{:S(2)}) collective-permute-start(bf16[2,6,6,13,128]{4,3,2,1,0:T(8,128)(2,1)S(1)} %get-tuple-element.20), channel_id=1, source_target_pairs={{0,8},{16,24},{32,40},{48,56},{64,72},{80,88},{96,104},{112,120},{... | collective-permute-start | bytes 718856 | tf_op jit(solution)/shard_map/ppermute | solution.py:459
  18.9 1.9 %collective-permute-start.1 = (bf16[2,6,6,13,128]{4,3,2,1,0:T(8,128)(2,1)S(1)}, bf16[2,6,6,13,128]{4,3,2,1,0:T(8,128)(2,1)S(1)}, u32[]{:S(2)}, u32[]{:S(2)}) collective-permute-start(bf16[2,6,6,13,128]{4,3,2,1,0:T(8,128)(2,1)S(1)} %get-tuple-element.21), channel_id=1, source_target_pairs={{8,16},{24,32},{40,48},{56,64},{72,80},{88,96},{104,112},{120,128}... | collective-permute-start | bytes 718856 | tf_op jit(solution)/shard_map/ppermute | solution.py:459
  20.8 0.0 copy-done
  20.8 0.0 copy-done.1
  20.8 0.0 copy-done.7
  20.8 3.8 %shard_map.86 = (bf16[6,6,6,13,128]{4,3,2,1,0:T(8,128)(2,1)}, bf16[6,6,6,13,128]{4,3,2,1,0:T(8,128)(2,1)}, bf16[2,2,6,6,13,128]{5,4,3,2,1,0:T(8,128)(2,1)}, bf16...) custom-call(bf16[6,6,6,13,128]{4,3,2,1,0:T(8,128)(2,1)S(1)} %bitcast.19, ...), custom_call_target="tpu_custom_call" | custom-call | flops 2147483648 | bytes 8388608 | tf_op jit(solution)/shard_map/pallas_call | solution.py:503
  24.6 0.0 all-to-all-done.bottom_ref
  24.6 0.0 copy-start.3
  24.7 0.0 copy-start.5
  24.7 1.2 %shard_map.87 = (bf16[2,6,6,13,128]{4,3,2,1,0:T(8,128)(2,1)S(1)}, bf16[2,16,128]{2,1,0:T(8,128)(2,1)S(1)}, f32[13,128]{1,0:T(8,128)S(1)}, s32[1,128]{1,0:T(1,128)S(1)}, s32[1,128]{1,0:T(1,128)S(1)}) custom-call(bf16[4,2,144,128]{3,2,1,0:T(8,128)(2,1)S(1)} %all-to-all-done.bottom_ref, bf16[6,6,6,13,128]{4,3,2,1,0:T(8,128)(2,1)} %bitcast.22, ...), custom_call_target="tpu_custom_call" | custom-call | flops 536870912 | bytes 4194304 | tf_op jit(solution)/shard_map/pallas_call | solution.py:534
  25.9 0.0 copy-start.2
  25.9 0.0 collective-permute-done.first_ref
  25.9 1.0 %collective-permute-done.1.second_ref = bf16[2,6,6,13,128]{4,3,2,1,0:T(8,128)(2,1)S(1)} collective-permute-done((bf16[2,6,6,13,128]{4,3,2,1,0:T(8,128)(2,1)S(1)}, bf16[2,6,6,13,128]{4,3,2,1,0:T(8,128)(2,1)S(1)}, u32[]{:S(2)}, u32[]{:S(2)}) %collective-permute-start.1) | collective-permute-done | bytes 239648 | tf_op jit(solution)/shard_map/ppermute | solution.py:459
  26.9 0.0 copy-start.4
  26.9 0.6 %shard_map.88 = bf16[8,64,128]{2,1,0:T(8,128)(2,1)S(1)} custom-call(bf16[2,6,6,13,128]{4,3,2,1,0:T(8,128)(2,1)S(1)} %collective-permute-done.first_ref, bf16[2,6,6,13,128]{4,3,2,1,0:T(8,128)(2,1)S(1)} %collective-permute-done.1.second_ref, bf16[2,6,6,13,128]{4,3,2,1,0:T(8,128)(2,1)S(1)} %get-tuple-element.24.lam_side_ref, ...), custom_call_target="tpu_custom_call" | custom-call | tf_op jit(solution)/shard_map/pallas_call | solution.py:557
  27.5 0.0 copy-start.6
  27.5 12.2 %all_to_all.10.got_ref = bf16[8,64,128]{2,1,0:T(8,128)(2,1)S(1)} all-to-all(bf16[8,64,128]{2,1,0:T(8,128)(2,1)S(1)} %shard_map.88), channel_id=1, replica_groups=mesh['layer'=4,'gx'=24,'gy'=8] {'gy'}, dimensions={0} | all-to-all | bytes 262144 | tf_op jit(solution)/shard_map/all_to_all | solution.py:566
  39.8 0.0 copy-done.3
  39.8 0.0 copy-done.5
  39.8 0.0 copy-done.2
  39.8 0.0 copy-done.4
  39.8 0.0 copy-done.6
  39.8 1.6 %shard_map.89 = (bf16[6,6,6,13,128]{4,3,2,1,0:T(8,128)(2,1)}, bf16[6,6,6,13,128]{4,3,2,1,0:T(8,128)(2,1)}, f32[13,1,128]{2,1,0:T(1,128)}) custom-call(bf16[8,64,128]{2,1,0:T(8,128)(2,1)S(1)} %all_to_all.10.got_ref, f32[7,16,128]{2,1,0:T(8,128)S(1)} %copy-done.6, ...), custom_call_target="tpu_custom_call", output_to_operand_aliasing={{0}: (11, {}), {1}: (12, {})} | custom-call | tf_op jit(solution)/shard_map/pallas_call | solution.py:568
Async XLA Ops:
  0.6 20.2 %copy-start = (bf16[13,1,1,6,6,6,128]{6,0,5,4,3,2,1:T(8,128)(2,1)S(1)}, bf16[13,1,1,6,6,6,128]{6,0,5,4,3,2,1:T(8,128)(2,1)}, u32[]{:S(2)}) copy-start(bf16[13,1,1,6,6,6,128]{6,0,5,4,3,2,1:T(8,128)(2,1)} %param.6) | copy-start | bytes 2156548
  0.6 20.2 %copy-start.1 = (bf16[13,1,1,6,6,6,128]{6,0,5,4,3,2,1:T(8,128)(2,1)S(1)}, bf16[13,1,1,6,6,6,128]{6,0,5,4,3,2,1:T(8,128)(2,1)}, u32[]{:S(2)}) copy-start(bf16[13,1,1,6,6,6,128]{6,0,5,4,3,2,1:T(8,128)(2,1)} %param.7) | copy-start | bytes 2156548
  2.9 17.9 %copy-start.7 = (f32[13,1,1,128]{3,2,1,0:T(1,128)S(1)}, f32[13,1,1,128]{3,2,1,0:T(1,128)}, u32[]{:S(2)}) copy-start(f32[13,1,1,128]{3,2,1,0:T(1,128)} %param.9) | copy-start | bytes 19972
  3.0 21.7 %all-to-all-start = ((bf16[4,2,144,128]{3,2,1,0:T(8,128)(2,1)}), bf16[4,2,144,128]{3,2,1,0:T(8,128)(2,1)S(1)}, u32[]{:S(2)}, u32[]{:S(2)}) async-start(bf16[4,2,144,128]{3,2,1,0:T(8,128)(2,1)} %get-tuple-element.22), calls=%async_computation | async-start | bytes 589824 | tf_op jit(solution)/shard_map/all_to_all | solution.py:499
  8.4 17.5 %collective-permute-start = (bf16[2,6,6,13,128]{4,3,2,1,0:T(8,128)(2,1)S(1)}, bf16[2,6,6,13,128]{4,3,2,1,0:T(8,128)(2,1)S(1)}, u32[]{:S(2)}, u32[]{:S(2)}) collective-permute-start(bf16[2,6,6,13,128]{4,3,2,1,0:T(8,128)(2,1)S(1)} %get-tuple-element.20), channel_id=1, source_target_pairs={{0,8},{16,24},{32,40},{48,56},{64,72},{80,88},{96,104},{112,120},{... | collective-permute-start | bytes 718856 | tf_op jit(solution)/shard_map/ppermute | solution.py:459
  18.9 8.0 %collective-permute-start.1 = (bf16[2,6,6,13,128]{4,3,2,1,0:T(8,128)(2,1)S(1)}, bf16[2,6,6,13,128]{4,3,2,1,0:T(8,128)(2,1)S(1)}, u32[]{:S(2)}, u32[]{:S(2)}) collective-permute-start(bf16[2,6,6,13,128]{4,3,2,1,0:T(8,128)(2,1)S(1)} %get-tuple-element.21), channel_id=1, source_target_pairs={{8,16},{24,32},{40,48},{56,64},{72,80},{88,96},{104,112},{120,128}... | collective-permute-start | bytes 718856 | tf_op jit(solution)/shard_map/ppermute | solution.py:459
  24.6 15.1 %copy-start.3 = (bf16[2,2,6,6,13,128]{5,4,3,2,1,0:T(8,128)(2,1)S(1)}, bf16[2,2,6,6,13,128]{5,4,3,2,1,0:T(8,128)(2,1)}, u32[]{:S(2)}) copy-start(bf16[2,2,6,6,13,128]{5,4,3,2,1,0:T(8,128)(2,1)} %get-tuple-element.29.side_ref) | copy-start | bytes 1437700
  24.7 15.1 %copy-start.5 = (bf16[2,4,6,13,128]{4,3,2,1,0:T(8,128)(2,1)S(1)}, bf16[2,4,6,13,128]{4,3,2,1,0:T(8,128)(2,1)}, u32[]{:S(2)}) copy-start(bf16[2,4,6,13,128]{4,3,2,1,0:T(8,128)(2,1)} %get-tuple-element.30.top_ref) | copy-start | bytes 479236
  25.9 13.9 %copy-start.2 = (bf16[13,1,1,6,6,6,128]{6,0,5,4,3,2,1:T(8,128)(2,1)S(1)}, bf16[13,1,1,6,6,6,128]{6,0,5,4,3,2,1:T(8,128)(2,1)}, u32[]{:S(2)}) copy-start(bf16[13,1,1,6,6,6,128]{6,0,5,4,3,2,1:T(8,128)(2,1)} %param.7) | copy-start | bytes 2156548
  26.9 12.9 %copy-start.4 = (bf16[2,4,2,5,13,128]{5,4,3,2,1,0:T(8,128)(2,1)S(1)}, bf16[2,4,2,5,13,128]{5,4,3,2,1,0:T(8,128)(2,1)}, u32[]{:S(2)}) copy-start(bf16[2,4,2,5,13,128]{5,4,3,2,1,0:T(8,128)(2,1)} %get-tuple-element.28.strip_ref) | copy-start | bytes 798724
  27.5 12.3 %copy-start.6 = (f32[7,16,128]{2,1,0:T(8,128)S(1)}, f32[7,16,128]{2,1,0:T(8,128)}, u32[]{:S(2)}) copy-start(f32[7,16,128]{2,1,0:T(8,128)} %get-tuple-element.23.small_hbm.small) | copy-start | bytes 172036

commit v2 on v1

--- a/solution.py
+++ b/solution.py
@@ -56,7 +56,7 @@
 
 def prep_kernel(
     wave_ref, adj_ref, stiff_ref, second_ref, first_ref, bottom_ref,
-    raw, kept, low, stiff, scale, rows, trace, sems,
+    raw, low, stiff, scale, rows, trace, sems,
 ):
     odd = lax.rem(lax.axis_index("gx"), 2)
     near = 5 * (1 - odd)
@@ -75,8 +75,7 @@
         send(adj_ref.at[far], raw.at[1]),
         send(adj_ref.at[near], raw.at[0]),
     ]
-    arrivals += [send(wave_ref.at[far], kept.at[1]), send(wave_ref.at[near], kept.at[0])]
-    leaving = []
+    leaving = [send(wave_ref.at[far], second_ref.at[0]), send(wave_ref.at[near], first_ref.at[0])]
     for copy in arrivals[0:3]:
         copy.wait()
     s = load_scale(stiff, scale)
@@ -92,9 +91,6 @@
         trace[part] = rows[...].astype(BF16)
     for group in range(bottom_ref.shape[0]):
         leaving.append(send(trace, bottom_ref.at[group]))
-    for out_ref, at in ((second_ref, 1), (first_ref, 0)):
-        arrivals[6 - at].wait()
-        leaving.append(send(kept.at[at], out_ref.at[0]))
     for out_ref, at in ((second_ref, 1), (first_ref, 0)):
         arrivals[4 - at].wait()
         for b in range(NP):
@@ -284,8 +280,8 @@
 
 def trace_kernel(
     bottom_ref, adj_hbm, partner_hbm, owner_hbm, small_hbm,
-    lam_side_ref, ends_ref, total_ref, owner_ref, mate_ref,
-    floors, partner_ref, small, lam_top, tile, sems,
+    lam_side_ref, lam_top, ends_ref, total_ref, owner_ref, mate_ref,
+    floors, partner_ref, small, tile, sems,
 ):
     copies = [
         pltpu.make_async_copy(src, dst, sems.at[i])
@@ -369,7 +365,7 @@
 
 def last_kernel(
     got_ref, small, strip_ref, side_ref, top_ref, second_ref, first_ref, bottom_ref, mate_ref,
-    wave_ref, adj_ref, old_wave_ref, old_adj_ref,
+    wave_ref, lam_side_ref, lam_top_ref, old_wave_ref, old_adj_ref,
     new_wave_ref, new_adj_ref, cell_ref,
     patched, side_new, top_new, cell, floors, sems,
 ):
@@ -389,7 +385,11 @@
     def finished(side, a, b, c):
         rate = (side_ref[side, a // 5, b, c] if a in (0, 5) else top_ref[side, a - 1, b]).astype(F32)
         rate = rate + TAU * outside(side, a, b, c, odd, first_ref, second_ref, floors.at[side])
-        return (adj_ref if side else wave_ref)[a, b, c].astype(F32) + factors[side] * rate
+        if side == 0:
+            old = wave_ref[a, b, c]
+        else:
+            old = lam_side_ref[a // 5, b, c] if a in (0, 5) else lam_top_ref[a, b]
+        return old.astype(F32) + factors[side] * rate
 
     for side, out_ref in ((0, new_wave_ref), (1, new_adj_ref)):
         load_floors(side, mate, bottom_ref, floors.at[side])
@@ -484,12 +484,11 @@
         scratch_shapes=[
             pltpu.VMEM((2, NP, NP, F, EY), BF16),
             pltpu.VMEM((2, NP, NP, F, EY), BF16),
-            pltpu.VMEM((2, NP, NP, F, EY), BF16),
             pltpu.VMEM((F, 1, EY), F32),
             pltpu.VMEM((ROWS, EY), F32),
             pltpu.VMEM((BOTTOM * NP * NP, EY), F32),
             pltpu.VMEM(traces.shape[1:], BF16),
-            pltpu.SemaphoreType.DMA((11 + layers,)),
+            pltpu.SemaphoreType.DMA((9 + layers,)),
         ],
         compiler_params=params,
     )(*far(wave, adj, stiff))
@@ -531,22 +530,22 @@
         cost_estimate=pl.CostEstimate(flops=2**31, bytes_accessed=2**23, transcendentals=0),
     )(wave, adj, stiff, *far(coup))
 
-    lam_sides, ends, total, own, mate = pl.pallas_call(
+    lam_sides, lam_tops, ends, total, own, mate = pl.pallas_call(
         trace_kernel,
         out_shape=(
             jax.ShapeDtypeStruct(side_shape[1:], BF16),
+            jax.ShapeDtypeStruct((NP, NP, F, EY), BF16),
             jax.ShapeDtypeStruct((2, ROWS, EY), BF16),
             jax.ShapeDtypeStruct((F, EY), F32),
             jax.ShapeDtypeStruct((1, EY), jnp.int32),
             jax.ShapeDtypeStruct((1, EY), jnp.int32),
         ),
         in_specs=[vmem] + [hbm] * 4,
-        out_specs=(vmem,) * 5,
+        out_specs=(vmem,) * 6,
         scratch_shapes=[
             pltpu.VMEM((NP * NP, F, EY), F32),
             pltpu.VMEM(partner.shape, jnp.int32),
             pltpu.VMEM(small_shape, F32),
-            pltpu.VMEM((NP, NP, F, EY), BF16),
             pltpu.VMEM((ROWS, EY), F32),
             pltpu.SemaphoreType.DMA((6,)),
         ],
@@ -568,7 +567,7 @@
     new_wave, new_adj, cells = pl.pallas_call(
         last_kernel,
         out_shape=(field, field, jax.ShapeDtypeStruct((F, 1, CELLS_DEV), F32)),
-        in_specs=[vmem] * 11 + [hbm] * 2,
+        in_specs=[vmem] * 12 + [hbm] * 2,
         out_specs=(hbm,) * 3,
         scratch_shapes=[
             pltpu.VMEM((2, 2, NP, NP, F, EY), BF16),
@@ -578,9 +577,9 @@
             pltpu.VMEM((2, NP * NP, F, EY), F32),
             pltpu.SemaphoreType.DMA((11,)),
         ],
-        input_output_aliases={11: 0, 12: 1},
+        input_output_aliases={12: 0, 13: 1},
         compiler_params=params,
-    )(got, small, strips, sides, tops, second, first, bottom, mate, wave, adj, new_wave, new_adj)
+    )(got, small, strips, sides, tops, second, first, bottom, mate, wave, lam_sides, lam_tops, new_wave, new_adj)
 
     new_wave = new_wave.transpose(3, 0, 1, 2, 4)[:, None, None]
     new_adj = new_adj.transpose(3, 0, 1, 2, 4)[:, None, None]

time: 41.8 us -> 41.5 us (level)
  no operation moved by 1% of the time
where the time goes in v2:
time: 41.5 us; the launch traced here: 41.1 us
  starting transfers between devices  17.8 us (43%)
  blocking collectives  12.2 us (29%)
  Pallas kernels  9.2 us (22%)
  waiting for transfers between devices  1.07 us (3%)
  between operations  0.76 us (2%)
    ppermute x2, starting transfers between devices, swap(): lax.ppermute(x, axis, [(i, j) for i, j in pairs] + [(j, i) for i, j in pa...  12.4 us
    all_to_all x1, blocking collectives, per_device(): got = lax.all_to_all(send, 'gy', 0, 0, tiled=True)  12.2 us
    all_to_all x1, starting transfers between devices, per_device(): bottom = lax.all_to_all(bottom, 'layer', 0, 0, tiled=True)  5.43 us
    pallas_call x1, Pallas kernels, per_device(): pl.pallas_call(inner_kernel, out_shape=(pltpu.HBM(field.shape, BF16), plt...  3.81 us
    pallas_call x1, Pallas kernels, per_device(): pl.pallas_call(prep_kernel, out_shape=(faces, faces, traces), in_specs=[h...  2.01 us
    pallas_call x1, Pallas kernels, per_device(): pl.pallas_call(last_kernel, out_shape=(field, field, jax.ShapeDtypeStruct...  1.61 us
    pallas_call x1, Pallas kernels, per_device(): pl.pallas_call(trace_kernel, out_shape=(jax.ShapeDtypeStruct(side_shape[1...  1.17 us
    ppermute x2, waiting for transfers between devices, swap(): lax.ppermute(x, axis, [(i, j) for i, j in pairs] + [(j, i) for i, j in pa...  1.07 us
  transfers between devices with their start and end apart: 3, of which 1 were waited for; matrix products, arithmetic and copies ran while one was open for 0% of the time, Pallas kernels for 12%

profile of v2, /device:TPU:1, one launch (start us, length us, event | category | flops | bytes accessed | tf_op | source)
XLA Modules:
  0.0 41.1 jit_solution(4523334609607975846)
XLA Ops:
  0.6 0.0 copy-start
  0.6 0.0 copy-start.1
  0.7 2.0 %shard_map.85 = (bf16[2,6,6,13,128]{4,3,2,1,0:T(8,128)(2,1)S(1)}, bf16[2,6,6,13,128]{4,3,2,1,0:T(8,128)(2,1)S(1)}, bf16[4,2,144,128]{3,2,1,0:T(8,128)(2,1)}) custom-call(bf16[6,6,6,13,128]{4,3,2,1,0:T(8,128)(2,1)} %bitcast.18, bf16[6,6,6,13,128]{4,3,2,1,0:T(8,128)(2,1)} %bitcast.21, f32[13,1,128]{2,1,0:T(1,128)} %bitcast.24), custom_call_target="tpu_custom_call" | custom-call | tf_op jit(solution)/shard_map/pallas_call | solution.py:479
  2.7 0.0 copy-start.6
  2.7 5.4 %all-to-all-start = ((bf16[4,2,144,128]{3,2,1,0:T(8,128)(2,1)}), bf16[4,2,144,128]{3,2,1,0:T(8,128)(2,1)S(1)}, u32[]{:S(2)}, u32[]{:S(2)}) async-start(bf16[4,2,144,128]{3,2,1,0:T(8,128)(2,1)} %get-tuple-element.23), calls=%async_computation | async-start | bytes 589824 | tf_op jit(solution)/shard_map/all_to_all | solution.py:498
  8.1 10.5 %collective-permute-start = (bf16[2,6,6,13,128]{4,3,2,1,0:T(8,128)(2,1)S(1)}, bf16[2,6,6,13,128]{4,3,2,1,0:T(8,128)(2,1)S(1)}, u32[]{:S(2)}, u32[]{:S(2)}) collective-permute-start(bf16[2,6,6,13,128]{4,3,2,1,0:T(8,128)(2,1)S(1)} %get-tuple-element.21), channel_id=1, source_target_pairs={{0,8},{16,24},{32,40},{48,56},{64,72},{80,88},{96,104},{112,120},{... | collective-permute-start | bytes 718856 | tf_op jit(solution)/shard_map/ppermute | solution.py:459
  18.6 1.9 %collective-permute-start.1 = (bf16[2,6,6,13,128]{4,3,2,1,0:T(8,128)(2,1)S(1)}, bf16[2,6,6,13,128]{4,3,2,1,0:T(8,128)(2,1)S(1)}, u32[]{:S(2)}, u32[]{:S(2)}) collective-permute-start(bf16[2,6,6,13,128]{4,3,2,1,0:T(8,128)(2,1)S(1)} %get-tuple-element.22), channel_id=1, source_target_pairs={{8,16},{24,32},{40,48},{56,64},{72,80},{88,96},{104,112},{120,128}... | collective-permute-start | bytes 718856 | tf_op jit(solution)/shard_map/ppermute | solution.py:459
  20.5 0.0 copy-done
  20.5 0.0 copy-done.1
  20.5 0.0 copy-done.6
  20.5 3.8 %shard_map.86 = (bf16[6,6,6,13,128]{4,3,2,1,0:T(8,128)(2,1)}, bf16[6,6,6,13,128]{4,3,2,1,0:T(8,128)(2,1)}, bf16[2,2,6,6,13,128]{5,4,3,2,1,0:T(8,128)(2,1)}, bf16...) custom-call(bf16[6,6,6,13,128]{4,3,2,1,0:T(8,128)(2,1)S(1)} %bitcast.19, ...), custom_call_target="tpu_custom_call" | custom-call | flops 2147483648 | bytes 8388608 | tf_op jit(solution)/shard_map/pallas_call | solution.py:502
  24.4 0.0 all-to-all-done.bottom_ref
  24.4 1.2 %shard_map.87 = (bf16[2,6,6,13,128]{4,3,2,1,0:T(8,128)(2,1)S(1)}, bf16[6,6,13,128]{3,2,1,0:T(8,128)(2,1)S(1)}, bf16[2,16,128]{2,1,0:T(8,128)(2,1)S(1)}, f32[13,1...) custom-call(bf16[4,2,144,128]{3,2,1,0:T(8,128)(2,1)S(1)} %all-to-all-done.bottom_ref, ...), custom_call_target="tpu_custom_call" | custom-call | flops 536870912 | bytes 4194304 | tf_op jit(solution)/shard_map/pallas_call | solution.py:533
  25.5 0.0 collective-permute-done.first_ref
  25.6 1.1 %collective-permute-done.1.second_ref = bf16[2,6,6,13,128]{4,3,2,1,0:T(8,128)(2,1)S(1)} collective-permute-done((bf16[2,6,6,13,128]{4,3,2,1,0:T(8,128)(2,1)S(1)}, bf16[2,6,6,13,128]{4,3,2,1,0:T(8,128)(2,1)S(1)}, u32[]{:S(2)}, u32[]{:S(2)}) %collective-permute-start.1) | collective-permute-done | bytes 239648 | tf_op jit(solution)/shard_map/ppermute | solution.py:459
  26.6 0.0 copy-start.2
  26.6 0.0 copy-start.3
  26.6 0.6 %shard_map.88 = bf16[8,64,128]{2,1,0:T(8,128)(2,1)S(1)} custom-call(bf16[2,6,6,13,128]{4,3,2,1,0:T(8,128)(2,1)S(1)} %collective-permute-done.first_ref, bf16[2,6,6,13,128]{4,3,2,1,0:T(8,128)(2,1)S(1)} %collective-permute-done.1.second_ref, bf16[2,6,6,13,128]{4,3,2,1,0:T(8,128)(2,1)S(1)} %get-tuple-element.25.lam_side_ref, ...), custom_call_target="tpu_custom_call" | custom-call | tf_op jit(solution)/shard_map/pallas_call | solution.py:556
  27.2 0.0 copy-start.4
  27.3 0.0 copy-start.5
  27.3 12.2 %all_to_all.10.got_ref = bf16[8,64,128]{2,1,0:T(8,128)(2,1)S(1)} all-to-all(bf16[8,64,128]{2,1,0:T(8,128)(2,1)S(1)} %shard_map.88), channel_id=1, replica_groups=mesh['layer'=4,'gx'=24,'gy'=8] {'gy'}, dimensions={0} | all-to-all | bytes 262144 | tf_op jit(solution)/shard_map/all_to_all | solution.py:565
  39.5 0.0 copy-done.2
  39.5 0.0 copy-done.3
  39.5 0.0 copy-done.4
  39.5 0.0 copy-done.5
  39.5 1.6 %shard_map.89 = (bf16[6,6,6,13,128]{4,3,2,1,0:T(8,128)(2,1)}, bf16[6,6,6,13,128]{4,3,2,1,0:T(8,128)(2,1)}, f32[13,1,128]{2,1,0:T(1,128)}) custom-call(bf16[8,64,128]{2,1,0:T(8,128)(2,1)S(1)} %all_to_all.10.got_ref, f32[7,16,128]{2,1,0:T(8,128)S(1)} %copy-done.5, ...), custom_call_target="tpu_custom_call", output_to_operand_aliasing={{0}: (12, {}), {1}: (13, {})} | custom-call | tf_op jit(solution)/shard_map/pallas_call | solution.py:567
Async XLA Ops:
  0.6 19.9 %copy-start = (bf16[13,1,1,6,6,6,128]{6,0,5,4,3,2,1:T(8,128)(2,1)S(1)}, bf16[13,1,1,6,6,6,128]{6,0,5,4,3,2,1:T(8,128)(2,1)}, u32[]{:S(2)}) copy-start(bf16[13,1,1,6,6,6,128]{6,0,5,4,3,2,1:T(8,128)(2,1)} %param.6) | copy-start | bytes 2156548
  0.6 19.9 %copy-start.1 = (bf16[13,1,1,6,6,6,128]{6,0,5,4,3,2,1:T(8,128)(2,1)S(1)}, bf16[13,1,1,6,6,6,128]{6,0,5,4,3,2,1:T(8,128)(2,1)}, u32[]{:S(2)}) copy-start(bf16[13,1,1,6,6,6,128]{6,0,5,4,3,2,1:T(8,128)(2,1)} %param.7) | copy-start | bytes 2156548
  2.7 17.9 %copy-start.6 = (f32[13,1,1,128]{3,2,1,0:T(1,128)S(1)}, f32[13,1,1,128]{3,2,1,0:T(1,128)}, u32[]{:S(2)}) copy-start(f32[13,1,1,128]{3,2,1,0:T(1,128)} %param.9) | copy-start | bytes 19972
  2.7 21.7 %all-to-all-start = ((bf16[4,2,144,128]{3,2,1,0:T(8,128)(2,1)}), bf16[4,2,144,128]{3,2,1,0:T(8,128)(2,1)S(1)}, u32[]{:S(2)}, u32[]{:S(2)}) async-start(bf16[4,2,144,128]{3,2,1,0:T(8,128)(2,1)} %get-tuple-element.23), calls=%async_computation | async-start | bytes 589824 | tf_op jit(solution)/shard_map/all_to_all | solution.py:498
  8.1 17.4 %collective-permute-start = (bf16[2,6,6,13,128]{4,3,2,1,0:T(8,128)(2,1)S(1)}, bf16[2,6,6,13,128]{4,3,2,1,0:T(8,128)(2,1)S(1)}, u32[]{:S(2)}, u32[]{:S(2)}) collective-permute-start(bf16[2,6,6,13,128]{4,3,2,1,0:T(8,128)(2,1)S(1)} %get-tuple-element.21), channel_id=1, source_target_pairs={{0,8},{16,24},{32,40},{48,56},{64,72},{80,88},{96,104},{112,120},{... | collective-permute-start | bytes 718856 | tf_op jit(solution)/shard_map/ppermute | solution.py:459
  18.6 8.0 %collective-permute-start.1 = (bf16[2,6,6,13,128]{4,3,2,1,0:T(8,128)(2,1)S(1)}, bf16[2,6,6,13,128]{4,3,2,1,0:T(8,128)(2,1)S(1)}, u32[]{:S(2)}, u32[]{:S(2)}) collective-permute-start(bf16[2,6,6,13,128]{4,3,2,1,0:T(8,128)(2,1)S(1)} %get-tuple-element.22), channel_id=1, source_target_pairs={{8,16},{24,32},{40,48},{56,64},{72,80},{88,96},{104,112},{120,128}... | collective-permute-start | bytes 718856 | tf_op jit(solution)/shard_map/ppermute | solution.py:459
  26.6 12.8 %copy-start.2 = (bf16[2,2,6,6,13,128]{5,4,3,2,1,0:T(8,128)(2,1)S(1)}, bf16[2,2,6,6,13,128]{5,4,3,2,1,0:T(8,128)(2,1)}, u32[]{:S(2)}) copy-start(bf16[2,2,6,6,13,128]{5,4,3,2,1,0:T(8,128)(2,1)} %get-tuple-element.30.side_ref) | copy-start | bytes 1437700
  26.6 12.8 %copy-start.3 = (bf16[2,4,2,5,13,128]{5,4,3,2,1,0:T(8,128)(2,1)S(1)}, bf16[2,4,2,5,13,128]{5,4,3,2,1,0:T(8,128)(2,1)}, u32[]{:S(2)}) copy-start(bf16[2,4,2,5,13,128]{5,4,3,2,1,0:T(8,128)(2,1)} %get-tuple-element.29.strip_ref) | copy-start | bytes 798724
  27.2 12.2 %copy-start.4 = (bf16[2,4,6,13,128]{4,3,2,1,0:T(8,128)(2,1)S(1)}, bf16[2,4,6,13,128]{4,3,2,1,0:T(8,128)(2,1)}, u32[]{:S(2)}) copy-start(bf16[2,4,6,13,128]{4,3,2,1,0:T(8,128)(2,1)} %get-tuple-element.31.top_ref) | copy-start | bytes 479236
  27.3 12.2 %copy-start.5 = (f32[7,16,128]{2,1,0:T(8,128)S(1)}, f32[7,16,128]{2,1,0:T(8,128)}, u32[]{:S(2)}) copy-start(f32[7,16,128]{2,1,0:T(8,128)} %get-tuple-element.24.small_hbm.small) | copy-start | bytes 172036

commit v3 on v1

--- a/solution.py
+++ b/solution.py
@@ -56,7 +56,7 @@
 
 def prep_kernel(
     wave_ref, adj_ref, stiff_ref, second_ref, first_ref, bottom_ref,
-    raw, kept, low, stiff, scale, rows, trace, sems,
+    raw, low, stiff, scale, rows, trace, sems,
 ):
     odd = lax.rem(lax.axis_index("gx"), 2)
     near = 5 * (1 - odd)
@@ -75,8 +75,7 @@
         send(adj_ref.at[far], raw.at[1]),
         send(adj_ref.at[near], raw.at[0]),
     ]
-    arrivals += [send(wave_ref.at[far], kept.at[1]), send(wave_ref.at[near], kept.at[0])]
-    leaving = []
+    leaving = [send(wave_ref.at[far], second_ref.at[0]), send(wave_ref.at[near], first_ref.at[0])]
     for copy in arrivals[0:3]:
         copy.wait()
     s = load_scale(stiff, scale)
@@ -92,9 +91,6 @@
         trace[part] = rows[...].astype(BF16)
     for group in range(bottom_ref.shape[0]):
         leaving.append(send(trace, bottom_ref.at[group]))
-    for out_ref, at in ((second_ref, 1), (first_ref, 0)):
-        arrivals[6 - at].wait()
-        leaving.append(send(kept.at[at], out_ref.at[0]))
     for out_ref, at in ((second_ref, 1), (first_ref, 0)):
         arrivals[4 - at].wait()
         for b in range(NP):
@@ -134,9 +130,9 @@
 
 
 def inner_kernel(
-    wave_ref, adj_ref, stiff_ref, coup_ref,
+    wave_ref, adj_ref, stiff_ref, coup_ref, partner_hbm, owner_hbm,
     new_wave_ref, new_adj_ref, side_out_ref, top_out_ref, strip_out_ref, small_out_ref,
-    scale, cs, mats, padded, packed, acc, mid, side_ref, top_ref, strip_ref, small, coup, sems,
+    scale, cs, mats, padded, packed, acc, mid, side_ref, top_ref, strip_ref, small, coup, partner_ref, owner_ref, sems,
 ):
     copies = []
 
@@ -145,7 +141,7 @@
         copies[-1].start()
         return copies[-1]
 
-    arrival = send(coup_ref, coup)
+    arrivals = [send(coup_ref, coup), send(partner_hbm, partner_ref), send(owner_hbm, owner_ref)]
     s = load_scale(stiff_ref, scale)
     for a in range(NP):
         padded[:, a, :, :, 8:ROWS, :] = jnp.zeros((2, NP, NP, ROWS - 8, EY), F32)
@@ -155,7 +151,10 @@
                 padded[1, a, b, c, 0:F, :] = adj_ref[a, b, c].astype(F32) * s
         for side in range(2):
             packed[side, a] = padded[side, a].astype(BF16)
-    arrival.wait()
+    for copy in arrivals:
+        copy.wait()
+    small[7, 0:1, :] = partner_ref[lax.axis_index("layer")].astype(F32)
+    small[7, 1:2, :] = owner_ref[...].astype(F32)
     small[0, 0:F, :] = s
 
     def leave(side, a):
@@ -173,7 +172,7 @@
             cs, mats, padded.at[side], packed.at[side], acc, mid, leave,
         )
     send(small, small_out_ref)
-    for copy in copies[1:]:
+    for copy in copies[3:]:
         copy.wait()
 
 
@@ -283,72 +282,60 @@
 
 
 def trace_kernel(
-    bottom_ref, adj_hbm, partner_hbm, owner_hbm, small_hbm,
-    lam_side_ref, ends_ref, total_ref, owner_ref, mate_ref,
-    floors, partner_ref, small, lam_top, tile, sems,
+    first_ref, bottom_ref, adj_ref, small_hbm,
+    ends_ref, total_ref, owner_ref, mate_ref,
+    floors, tile, small, sem,
 ):
-    copies = [
-        pltpu.make_async_copy(src, dst, sems.at[i])
-        for i, (src, dst) in enumerate(
-            (
-                (partner_hbm, partner_ref),
-                (adj_hbm.at[:, :, 5], lam_top),
-                (small_hbm, small),
-                (owner_hbm, owner_ref),
-                (adj_hbm.at[0], lam_side_ref.at[0]),
-                (adj_hbm.at[5], lam_side_ref.at[1]),
-            )
-        )
-    ]
-    for copy in copies:
-        copy.start()
-    copies[0].wait()
-    mate = partner_ref[lax.axis_index("layer")]
+    arrival = pltpu.make_async_copy(small_hbm, small, sem)
+    arrival.start()
+    floors[...] = jnp.zeros_like(floors)
+    near = 5 * (1 - lax.rem(lax.axis_index("gx"), 2))
+    sides = jnp.zeros((F, EY), F32)
+    for b in range(NP):
+        for c in range(NP):
+            sides = sides + adj_ref[near, b, c].astype(F32) * first_ref[0, b, c].astype(F32)
+    arrival.wait()
+    mate = small[7, 0:1, :].astype(jnp.int32)
     mate_ref[...] = mate
-    floors[...] = jnp.zeros_like(floors)
+    owner_ref[...] = small[7, 1:2, :].astype(jnp.int32)
     load_floors(0, mate, bottom_ref, floors)
-    copies[1].wait()
     total = jnp.zeros((F, EY), F32)
     row_ids = lax.broadcasted_iota(jnp.int32, (F, EY), 0)
     for a in range(NP):
         for b in range(NP):
-            total = total + lam_top[a, b].astype(F32) * floors[a * NP + b]
-    copies[2].wait()
-    total_ref[...] = small[3, 0:F, :] + jnp.where(row_ids < BOTTOM, TAU * total, 0.0)
+            total = total + adj_ref[a, b, 5].astype(F32) * floors[a * NP + b]
+    total = jnp.where(row_ids < BOTTOM, total, 0.0) + sides
+    total_ref[...] = small[3, 0:F, :] + TAU * total
     tile[...] = jnp.zeros_like(tile)
     for i in range(2):
         tile[0:F, :] = small[4 + i, 0:F, :]
         ends_ref[i] = tile[...].astype(BF16)
-    for copy in copies[3:]:
-        copy.wait()
 
 
 def outer_kernel(
-    first_ref, second_ref, lam_side_ref, ends_ref, total_ref, owner_ref,
+    second_ref, adj_ref, ends_ref, total_ref, owner_ref,
     send_ref,
     tile,
 ):
-    odd = lax.rem(lax.axis_index("gx"), 2) == 1
+    far = 5 * lax.rem(lax.axis_index("gx"), 2)
     total = jnp.zeros((F, EY), F32)
     for b in range(NP):
         for c in range(NP):
-            one, two = first_ref[0, b, c].astype(F32), second_ref[0, b, c].astype(F32)
-            low, high = jnp.where(odd, one, two), jnp.where(odd, two, one)
-            total = total + lam_side_ref[0, b, c].astype(F32) * low
-            total = total + lam_side_ref[1, b, c].astype(F32) * high
-    total = total_ref[...] + TAU * total
-    total = DT * total
+            total = total + adj_ref[far, b, c].astype(F32) * second_ref[0, b, c].astype(F32)
+    tile[...] = jnp.zeros_like(tile)
+    tile[0:F, :] = DT * (total_ref[...] + TAU * total)
+    total = tile[...]
     high = total.astype(BF16)
     rest = total - high.astype(F32)
     middle = rest.astype(BF16)
     low = (rest - middle.astype(F32)).astype(BF16)
+    parts = jnp.concatenate([low, middle, high], axis=0)
     owner = owner_ref[0]
     count = send_ref.shape[0]
     lane = lane_ids(1)
     own_left = jnp.sum(jnp.where(lane == 0, owner, 0), axis=1, keepdims=True).astype(F32)
     own_right = jnp.sum(jnp.where(lane == EY - 1, owner, 0), axis=1, keepdims=True).astype(F32)
     zeros = jnp.zeros((1, EY), F32)
-    tile[...] = jnp.zeros_like(tile)
     for i in range(2):
         for target in range(count):
             send_ref[target, (2 + i) * ROWS : (3 + i) * ROWS, :] = ends_ref[i]
@@ -357,10 +344,9 @@
     for target in range(count):
         cells = lax.broadcasted_iota(jnp.int32, (CELLS_DEV, EY), 0) + CELLS_DEV * target
         held = (cells == owner).astype(BF16)
-        tile[0:F, :] = sum(
-            lax.dot_general(x, held, (((1,), (1,)), ((), ())), preferred_element_type=F32)
-            for x in (low, middle, high)
-        )
+        sums = lax.dot_general(parts, held, (((1,), (1,)), ((), ())), preferred_element_type=F32)
+        sums = sums[0:ROWS] + sums[ROWS : 2 * ROWS] + sums[2 * ROWS :]
+        tile[0:F, :] = sums[0:F]
         whole = tile[...]
         top = whole.astype(BF16)
         send_ref[target, 0:ROWS, :] = top
@@ -484,12 +470,11 @@
         scratch_shapes=[
             pltpu.VMEM((2, NP, NP, F, EY), BF16),
             pltpu.VMEM((2, NP, NP, F, EY), BF16),
-            pltpu.VMEM((2, NP, NP, F, EY), BF16),
             pltpu.VMEM((F, 1, EY), F32),
             pltpu.VMEM((ROWS, EY), F32),
             pltpu.VMEM((BOTTOM * NP * NP, EY), F32),
             pltpu.VMEM(traces.shape[1:], BF16),
-            pltpu.SemaphoreType.DMA((11 + layers,)),
+            pltpu.SemaphoreType.DMA((9 + layers,)),
         ],
         compiler_params=params,
     )(*far(wave, adj, stiff))
@@ -499,7 +484,7 @@
     bottom = lax.all_to_all(bottom, "layer", 0, 0, tiled=True)
 
     side_shape, top_shape, strip_shape = (2, 2, NP, NP, F, EY), (2, 4, NP, F, EY), (2, 4, 2, 5, F, EY)
-    small_shape = (7, ROWS, EY)
+    small_shape = (8, ROWS, EY)
     new_wave, new_adj, sides, tops, strips, small = pl.pallas_call(
         inner_kernel,
         out_shape=(
@@ -510,7 +495,7 @@
             pltpu.HBM(strip_shape, BF16),
             pltpu.HBM(small_shape, F32),
         ),
-        in_specs=[vmem] * 3 + [hbm],
+        in_specs=[vmem] * 3 + [hbm] * 3,
         out_specs=(hbm,) * 6,
         scratch_shapes=[
             pltpu.VMEM((ROWS, EY), F32),
@@ -525,43 +510,42 @@
             pltpu.VMEM(strip_shape, BF16),
             pltpu.VMEM(small_shape, F32),
             pltpu.VMEM(coup.shape, F32),
-            pltpu.SemaphoreType.DMA((30,)),
+            pltpu.VMEM(partner.shape, jnp.int32),
+            pltpu.VMEM(own.shape, jnp.int32),
+            pltpu.SemaphoreType.DMA((32,)),
         ],
         compiler_params=params,
         cost_estimate=pl.CostEstimate(flops=2**31, bytes_accessed=2**23, transcendentals=0),
-    )(wave, adj, stiff, *far(coup))
-
-    lam_sides, ends, total, own, mate = pl.pallas_call(
+    )(wave, adj, stiff, *far(coup, partner, own))
+
+    ends, total, own, mate = pl.pallas_call(
         trace_kernel,
         out_shape=(
-            jax.ShapeDtypeStruct(side_shape[1:], BF16),
             jax.ShapeDtypeStruct((2, ROWS, EY), BF16),
             jax.ShapeDtypeStruct((F, EY), F32),
             jax.ShapeDtypeStruct((1, EY), jnp.int32),
             jax.ShapeDtypeStruct((1, EY), jnp.int32),
         ),
-        in_specs=[vmem] + [hbm] * 4,
-        out_specs=(vmem,) * 5,
+        in_specs=[vmem] * 3 + [hbm],
+        out_specs=(vmem,) * 4,
         scratch_shapes=[
             pltpu.VMEM((NP * NP, F, EY), F32),
-            pltpu.VMEM(partner.shape, jnp.int32),
+            pltpu.VMEM((ROWS, EY), F32),
             pltpu.VMEM(small_shape, F32),
-            pltpu.VMEM((NP, NP, F, EY), BF16),
-            pltpu.VMEM((ROWS, EY), F32),
-            pltpu.SemaphoreType.DMA((6,)),
+            pltpu.SemaphoreType.DMA,
         ],
         compiler_params=params,
         cost_estimate=pl.CostEstimate(flops=2**29, bytes_accessed=2**22, transcendentals=0),
-    )(bottom, *far(adj, partner, own, small))
+    )(first, bottom, adj, *far(small))
 
     send = pl.pallas_call(
         outer_kernel,
         out_shape=jax.ShapeDtypeStruct((count, 4 * ROWS, EY), BF16),
-        in_specs=[vmem] * 6,
+        in_specs=[vmem] * 5,
         out_specs=vmem,
         scratch_shapes=[pltpu.VMEM((ROWS, EY), F32)],
         compiler_params=params,
-    )(first, second, lam_sides, ends, total, own)
+    )(second, adj, ends, total, own)
 
     got = lax.all_to_all(send, "gy", 0, 0, tiled=True)
 

time: 41.8 us -> 41.1 us (0.983)
  Pallas kernels: 9.56 us -> 8.65 us
where the time goes in v3:
time: 41.1 us; the launch traced here: 40.6 us
  starting transfers between devices  17.8 us (43%)
  blocking collectives  12 us (29%)
  Pallas kernels  8.65 us (21%)
  waiting for transfers between devices  1.3 us (3%)
  between operations  0.76 us (2%)
    ppermute x2, starting transfers between devices, swap(): lax.ppermute(x, axis, [(i, j) for i, j in pairs] + [(j, i) for i, j in pa...  12.4 us
    all_to_all x1, blocking collectives, per_device(): got = lax.all_to_all(send, 'gy', 0, 0, tiled=True)  12 us
    all_to_all x1, starting transfers between devices, per_device(): bottom = lax.all_to_all(bottom, 'layer', 0, 0, tiled=True)  5.43 us
    pallas_call x1, Pallas kernels, per_device(): pl.pallas_call(inner_kernel, out_shape=(pltpu.HBM(field.shape, BF16), plt...  3.83 us
    pallas_call x1, Pallas kernels, per_device(): pl.pallas_call(prep_kernel, out_shape=(faces, faces, traces), in_specs=[h...  2.01 us
    pallas_call x1, Pallas kernels, per_device(): pl.pallas_call(last_kernel, out_shape=(field, field, jax.ShapeDtypeStruct...  1.59 us
    ppermute x2, waiting for transfers between devices, swap(): lax.ppermute(x, axis, [(i, j) for i, j in pairs] + [(j, i) for i, j in pa...  1.3 us
    pallas_call x1, Pallas kernels, per_device(): pl.pallas_call(trace_kernel, out_shape=(jax.ShapeDtypeStruct((2, ROWS, EY...  0.92 us
  transfers between devices with their start and end apart: 3, of which 1 were waited for; matrix products, arithmetic and copies ran while one was open for 0% of the time, Pallas kernels for 12%

profile of v3, /device:TPU:1, one launch (start us, length us, event | category | flops | bytes accessed | tf_op | source)
XLA Modules:
  0.0 40.6 jit_solution(8812214310063038550)
XLA Ops:
  0.6 0.0 copy-start
  0.6 0.0 copy-start.1
  0.6 2.0 %shard_map.85 = (bf16[2,6,6,13,128]{4,3,2,1,0:T(8,128)(2,1)S(1)}, bf16[2,6,6,13,128]{4,3,2,1,0:T(8,128)(2,1)S(1)}, bf16[4,2,144,128]{3,2,1,0:T(8,128)(2,1)}) custom-call(bf16[6,6,6,13,128]{4,3,2,1,0:T(8,128)(2,1)} %bitcast.23, bf16[6,6,6,13,128]{4,3,2,1,0:T(8,128)(2,1)} %bitcast.18, f32[13,1,128]{2,1,0:T(1,128)} %bitcast.26), custom_call_target="tpu_custom_call" | custom-call | tf_op jit(solution)/shard_map/pallas_call | solution.py:465
  2.7 5.4 %all-to-all-start = ((bf16[4,2,144,128]{3,2,1,0:T(8,128)(2,1)}), bf16[4,2,144,128]{3,2,1,0:T(8,128)(2,1)S(1)}, u32[]{:S(2)}, u32[]{:S(2)}) async-start(bf16[4,2,144,128]{3,2,1,0:T(8,128)(2,1)} %get-tuple-element.21), calls=%async_computation | async-start | bytes 589824 | tf_op jit(solution)/shard_map/all_to_all | solution.py:484
  8.1 0.0 copy-start.6
  8.1 10.5 %collective-permute-start.1 = (bf16[2,6,6,13,128]{4,3,2,1,0:T(8,128)(2,1)S(1)}, bf16[2,6,6,13,128]{4,3,2,1,0:T(8,128)(2,1)S(1)}, u32[]{:S(2)}, u32[]{:S(2)}) collective-permute-start(bf16[2,6,6,13,128]{4,3,2,1,0:T(8,128)(2,1)S(1)} %get-tuple-element.20), channel_id=1, source_target_pairs={{0,8},{16,24},{32,40},{48,56},{64,72},{80,88},{96,104},{112,120},{... | collective-permute-start | bytes 718856 | tf_op jit(solution)/shard_map/ppermute | solution.py:445
  18.6 1.9 %collective-permute-start = (bf16[2,6,6,13,128]{4,3,2,1,0:T(8,128)(2,1)S(1)}, bf16[2,6,6,13,128]{4,3,2,1,0:T(8,128)(2,1)S(1)}, u32[]{:S(2)}, u32[]{:S(2)}) collective-permute-start(bf16[2,6,6,13,128]{4,3,2,1,0:T(8,128)(2,1)S(1)} %get-tuple-element.19), channel_id=1, source_target_pairs={{8,16},{24,32},{40,48},{56,64},{72,80},{88,96},{104,112},{120,128}... | collective-permute-start | bytes 718856 | tf_op jit(solution)/shard_map/ppermute | solution.py:445
  20.5 0.0 copy-done
  20.5 0.0 copy-done.1
  20.5 0.0 copy-done.6
  20.5 3.8 %shard_map.86 = (bf16[6,6,6,13,128]{4,3,2,1,0:T(8,128)(2,1)}, bf16[6,6,6,13,128]{4,3,2,1,0:T(8,128)(2,1)}, bf16[2,2,6,6,13,128]{5,4,3,2,1,0:T(8,128)(2,1)}, bf16...) custom-call(bf16[6,6,6,13,128]{4,3,2,1,0:T(8,128)(2,1)S(1)} %bitcast.24, ...), custom_call_target="tpu_custom_call" | custom-call | flops 2147483648 | bytes 8388608 | tf_op jit(solution)/shard_map/pallas_call | solution.py:488
  24.4 0.0 collective-permute-done.1.first_ref
  24.4 0.0 all-to-all-done.bottom_ref
  24.4 0.9 %shard_map.87 = (bf16[2,16,128]{2,1,0:T(8,128)(2,1)S(1)}, f32[13,128]{1,0:T(8,128)S(1)}, s32[1,128]{1,0:T(1,128)S(1)}, s32[1,128]{1,0:T(1,128)S(1)}) custom-call(bf16[2,6,6,13,128]{4,3,2,1,0:T(8,128)(2,1)S(1)} %collective-permute-done.1.first_ref, bf16[4,2,144,128]{3,2,1,0:T(8,128)(2,1)S(1)} %all-to-all-done.bottom_ref, ...), custom_call_target="tpu_custom_call" | custom-call | flops 536870912 | bytes 4194304 | tf_op jit(solution)/shard_map/pallas_call | solution.py:521
  25.3 1.3 %collective-permute-done.second_ref = bf16[2,6,6,13,128]{4,3,2,1,0:T(8,128)(2,1)S(1)} collective-permute-done((bf16[2,6,6,13,128]{4,3,2,1,0:T(8,128)(2,1)S(1)}, bf16[2,6,6,13,128]{4,3,2,1,0:T(8,128)(2,1)S(1)}, u32[]{:S(2)}, u32[]{:S(2)}) %collective-permute-start) | collective-permute-done | bytes 239648 | tf_op jit(solution)/shard_map/ppermute | solution.py:445
  26.6 0.0 copy-start.2
  26.6 0.0 copy-start.3
  26.6 0.3 shard_map.88
  26.9 0.0 copy-start.4
  27.0 0.0 copy-start.5
  27.0 12.0 %all_to_all.10.got_ref = bf16[8,64,128]{2,1,0:T(8,128)(2,1)S(1)} all-to-all(bf16[8,64,128]{2,1,0:T(8,128)(2,1)S(1)} %shard_map.88), channel_id=1, replica_groups=mesh['layer'=4,'gx'=24,'gy'=8] {'gy'}, dimensions={0} | all-to-all | bytes 262144 | tf_op jit(solution)/shard_map/all_to_all | solution.py:550
  39.0 0.0 copy-done.2
  39.0 0.0 copy-done.3
  39.0 0.0 copy-done.4
  39.0 0.0 copy-done.5
  39.0 1.6 %shard_map.89 = (bf16[6,6,6,13,128]{4,3,2,1,0:T(8,128)(2,1)}, bf16[6,6,6,13,128]{4,3,2,1,0:T(8,128)(2,1)}, f32[13,1,128]{2,1,0:T(1,128)}) custom-call(bf16[8,64,128]{2,1,0:T(8,128)(2,1)S(1)} %all_to_all.10.got_ref, f32[8,16,128]{2,1,0:T(8,128)S(1)} %copy-done.5, ...), custom_call_target="tpu_custom_call", output_to_operand_aliasing={{0}: (11, {}), {1}: (12, {})} | custom-call | tf_op jit(solution)/shard_map/pallas_call | solution.py:552
Async XLA Ops:
  0.6 19.9 %copy-start = (bf16[13,1,1,6,6,6,128]{6,0,5,4,3,2,1:T(8,128)(2,1)S(1)}, bf16[13,1,1,6,6,6,128]{6,0,5,4,3,2,1:T(8,128)(2,1)}, u32[]{:S(2)}) copy-start(bf16[13,1,1,6,6,6,128]{6,0,5,4,3,2,1:T(8,128)(2,1)} %param.7) | copy-start | bytes 2156548
  0.6 19.9 %copy-start.1 = (bf16[13,1,1,6,6,6,128]{6,0,5,4,3,2,1:T(8,128)(2,1)S(1)}, bf16[13,1,1,6,6,6,128]{6,0,5,4,3,2,1:T(8,128)(2,1)}, u32[]{:S(2)}) copy-start(bf16[13,1,1,6,6,6,128]{6,0,5,4,3,2,1:T(8,128)(2,1)} %param.6) | copy-start | bytes 2156548
  2.7 21.7 %all-to-all-start = ((bf16[4,2,144,128]{3,2,1,0:T(8,128)(2,1)}), bf16[4,2,144,128]{3,2,1,0:T(8,128)(2,1)S(1)}, u32[]{:S(2)}, u32[]{:S(2)}) async-start(bf16[4,2,144,128]{3,2,1,0:T(8,128)(2,1)} %get-tuple-element.21), calls=%async_computation | async-start | bytes 589824 | tf_op jit(solution)/shard_map/all_to_all | solution.py:484
  8.1 12.4 %copy-start.6 = (f32[13,1,1,128]{3,2,1,0:T(1,128)S(1)}, f32[13,1,1,128]{3,2,1,0:T(1,128)}, u32[]{:S(2)}) copy-start(f32[13,1,1,128]{3,2,1,0:T(1,128)} %param.9) | copy-start | bytes 19972
  8.1 16.3 %collective-permute-start.1 = (bf16[2,6,6,13,128]{4,3,2,1,0:T(8,128)(2,1)S(1)}, bf16[2,6,6,13,128]{4,3,2,1,0:T(8,128)(2,1)S(1)}, u32[]{:S(2)}, u32[]{:S(2)}) collective-permute-start(bf16[2,6,6,13,128]{4,3,2,1,0:T(8,128)(2,1)S(1)} %get-tuple-element.20), channel_id=1, source_target_pairs={{0,8},{16,24},{32,40},{48,56},{64,72},{80,88},{96,104},{112,120},{... | collective-permute-start | bytes 718856 | tf_op jit(solution)/shard_map/ppermute | solution.py:445
  18.6 8.0 %collective-permute-start = (bf16[2,6,6,13,128]{4,3,2,1,0:T(8,128)(2,1)S(1)}, bf16[2,6,6,13,128]{4,3,2,1,0:T(8,128)(2,1)S(1)}, u32[]{:S(2)}, u32[]{:S(2)}) collective-permute-start(bf16[2,6,6,13,128]{4,3,2,1,0:T(8,128)(2,1)S(1)} %get-tuple-element.19), channel_id=1, source_target_pairs={{8,16},{24,32},{40,48},{56,64},{72,80},{88,96},{104,112},{120,128}... | collective-permute-start | bytes 718856 | tf_op jit(solution)/shard_map/ppermute | solution.py:445
  26.6 12.3 %copy-start.2 = (bf16[2,2,6,6,13,128]{5,4,3,2,1,0:T(8,128)(2,1)S(1)}, bf16[2,2,6,6,13,128]{5,4,3,2,1,0:T(8,128)(2,1)}, u32[]{:S(2)}) copy-start(bf16[2,2,6,6,13,128]{5,4,3,2,1,0:T(8,128)(2,1)} %get-tuple-element.27.side_ref) | copy-start | bytes 1437700
  26.6 12.3 %copy-start.3 = (bf16[2,4,2,5,13,128]{5,4,3,2,1,0:T(8,128)(2,1)S(1)}, bf16[2,4,2,5,13,128]{5,4,3,2,1,0:T(8,128)(2,1)}, u32[]{:S(2)}) copy-start(bf16[2,4,2,5,13,128]{5,4,3,2,1,0:T(8,128)(2,1)} %get-tuple-element.26.strip_ref) | copy-start | bytes 798724
  26.9 12.0 %copy-start.4 = (bf16[2,4,6,13,128]{4,3,2,1,0:T(8,128)(2,1)S(1)}, bf16[2,4,6,13,128]{4,3,2,1,0:T(8,128)(2,1)}, u32[]{:S(2)}) copy-start(bf16[2,4,6,13,128]{4,3,2,1,0:T(8,128)(2,1)} %get-tuple-element.28.top_ref) | copy-start | bytes 479236
  27.0 12.0 %copy-start.5 = (f32[8,16,128]{2,1,0:T(8,128)S(1)}, f32[8,16,128]{2,1,0:T(8,128)}, u32[]{:S(2)}) copy-start(f32[8,16,128]{2,1,0:T(8,128)} %get-tuple-element.22.small_hbm.small) | copy-start | bytes 196612

commit v4 on v3

--- a/solution.py
+++ b/solution.py
@@ -333,24 +333,20 @@
     owner = owner_ref[0]
     count = send_ref.shape[0]
     lane = lane_ids(1)
-    own_left = jnp.sum(jnp.where(lane == 0, owner, 0), axis=1, keepdims=True).astype(F32)
-    own_right = jnp.sum(jnp.where(lane == EY - 1, owner, 0), axis=1, keepdims=True).astype(F32)
-    zeros = jnp.zeros((1, EY), F32)
+    own_left = jnp.sum(jnp.where(lane == 0, owner, 0), axis=1, keepdims=True)
+    own_right = jnp.sum(jnp.where(lane == EY - 1, owner, 0), axis=1, keepdims=True)
     for i in range(2):
         for target in range(count):
-            send_ref[target, (2 + i) * ROWS : (3 + i) * ROWS, :] = ends_ref[i]
-    tile[F : F + 1, :] = zeros + own_left
-    tile[F + 1 : F + 2, :] = zeros + own_right
+            send_ref[target, (1 + i) * ROWS : (2 + i) * ROWS, :] = ends_ref[i]
+    for i, own in enumerate((own_left, own_right)):
+        tile[F + i : F + i + 1, :] = jnp.where(lane < HALF, own >> 7, own & 127).astype(F32)
     for target in range(count):
         cells = lax.broadcasted_iota(jnp.int32, (CELLS_DEV, EY), 0) + CELLS_DEV * target
         held = (cells == owner).astype(BF16)
         sums = lax.dot_general(parts, held, (((1,), (1,)), ((), ())), preferred_element_type=F32)
         sums = sums[0:ROWS] + sums[ROWS : 2 * ROWS] + sums[2 * ROWS :]
         tile[0:F, :] = sums[0:F]
-        whole = tile[...]
-        top = whole.astype(BF16)
-        send_ref[target, 0:ROWS, :] = top
-        send_ref[target, ROWS : 2 * ROWS, :] = (whole - top.astype(F32)).astype(BF16)
+        send_ref[target, 0:ROWS, :] = tile[...].astype(BF16)
 
 
 def last_kernel(
@@ -396,16 +392,18 @@
         return got_ref[j, ROWS * i : ROWS * (i + 1), :].astype(F32)
 
     cells = jnp.zeros((F, EY), F32)
-    lane = (lane_ids(1) + CELLS_DEV * me).astype(F32)
+    lane = lane_ids(1).astype(F32)
     for j in range(count):
-        sums = tile(j, 0) + tile(j, 1)
+        sums = tile(j, 0)
         cells = cells + sums[0:F]
-        lam = tile(j, 3)[0:F]
+        lam = tile(j, 2)[0:F]
         for other, side, row in ((j - 1, upper, F), (j + 1, lanes < HALF, F + 1)):
             if 0 <= other < count:
-                pairs = jnp.where(side, lam * tile(other, 2)[0:F], 0.0)
+                pairs = jnp.where(side, lam * tile(other, 1)[0:F], 0.0)
                 value = (DT * TAU) * jnp.sum(pairs, axis=1, keepdims=True)
-                cells = cells + jnp.where(sums[row : row + 1] == lane, value, 0.0)
+                place = sums[row : row + 1]
+                hit = (place[:, 0:1] == me.astype(F32)) & (place[:, HALF : HALF + 1] == lane)
+                cells = cells + jnp.where(hit, value, 0.0)
     for f in range(F):
         cell[f] = cells[f : f + 1]
     send(cell, cell_ref)
@@ -417,8 +415,8 @@
         return jnp.sum(jnp.where(lanes == column, values, 0.0), axis=1, keepdims=True)
 
     for side, out_ref in ((0, new_wave_ref), (1, new_adj_ref)):
-        low = jnp.where(me > 0, tile(below, 2 + side)[0:F], 0.0)
-        high = jnp.where(me < count - 1, tile(above, 2 + side)[0:F], 0.0)
+        low = jnp.where(me > 0, tile(below, 1 + side)[0:F], 0.0)
+        high = jnp.where(me < count - 1, tile(above, 1 + side)[0:F], 0.0)
         if side == 0:
             near = jnp.where(upper, low, high) * small[6, 0:F, :]
         else:
@@ -540,7 +538,7 @@
 
     send = pl.pallas_call(
         outer_kernel,
-        out_shape=jax.ShapeDtypeStruct((count, 4 * ROWS, EY), BF16),
+        out_shape=jax.ShapeDtypeStruct((count, 3 * ROWS, EY), BF16),
         in_specs=[vmem] * 5,
         out_specs=vmem,
         scratch_shapes=[pltpu.VMEM((ROWS, EY), F32)],

time: 41.1 us -> 40.8 us (level)
  no operation moved by 1% of the time
where the time goes in v4:
time: 40.8 us; the launch traced here: 40.4 us
  starting transfers between devices  17.8 us (44%)
  blocking collectives  11.8 us (29%)
  Pallas kernels  8.68 us (21%)
  waiting for transfers between devices  1.3 us (3%)
  between operations  0.76 us (2%)
    ppermute x2, starting transfers between devices, swap(): lax.ppermute(x, axis, [(i, j) for i, j in pairs] + [(j, i) for i, j in pa...  12.4 us
    all_to_all x1, blocking collectives, per_device(): got = lax.all_to_all(send, 'gy', 0, 0, tiled=True)  11.8 us
    all_to_all x1, starting transfers between devices, per_device(): bottom = lax.all_to_all(bottom, 'layer', 0, 0, tiled=True)  5.43 us
    pallas_call x1, Pallas kernels, per_device(): pl.pallas_call(inner_kernel, out_shape=(pltpu.HBM(field.shape, BF16), plt...  3.83 us
    pallas_call x1, Pallas kernels, per_device(): pl.pallas_call(prep_kernel, out_shape=(faces, faces, traces), in_specs=[h...  2.01 us
    pallas_call x1, Pallas kernels, per_device(): pl.pallas_call(last_kernel, out_shape=(field, field, jax.ShapeDtypeStruct...  1.64 us
    ppermute x2, waiting for transfers between devices, swap(): lax.ppermute(x, axis, [(i, j) for i, j in pairs] + [(j, i) for i, j in pa...  1.3 us
    pallas_call x1, Pallas kernels, per_device(): pl.pallas_call(trace_kernel, out_shape=(jax.ShapeDtypeStruct((2, ROWS, EY...  0.92 us
  transfers between devices with their start and end apart: 3, of which 1 were waited for; matrix products, arithmetic and copies ran while one was open for 0% of the time, Pallas kernels for 12%

profile of v4, /device:TPU:1, one launch (start us, length us, event | category | flops | bytes accessed | tf_op | source)
XLA Modules:
  0.0 40.4 jit_solution(16760132485239847462)
XLA Ops:
  0.6 0.0 copy-start
  0.6 0.0 copy-start.1
  0.6 2.0 %shard_map.85 = (bf16[2,6,6,13,128]{4,3,2,1,0:T(8,128)(2,1)S(1)}, bf16[2,6,6,13,128]{4,3,2,1,0:T(8,128)(2,1)S(1)}, bf16[4,2,144,128]{3,2,1,0:T(8,128)(2,1)}) custom-call(bf16[6,6,6,13,128]{4,3,2,1,0:T(8,128)(2,1)} %bitcast.23, bf16[6,6,6,13,128]{4,3,2,1,0:T(8,128)(2,1)} %bitcast.18, f32[13,1,128]{2,1,0:T(1,128)} %bitcast.26), custom_call_target="tpu_custom_call" | custom-call | tf_op jit(solution)/shard_map/pallas_call | solution.py:463
  2.7 5.4 %all-to-all-start = ((bf16[4,2,144,128]{3,2,1,0:T(8,128)(2,1)}), bf16[4,2,144,128]{3,2,1,0:T(8,128)(2,1)S(1)}, u32[]{:S(2)}, u32[]{:S(2)}) async-start(bf16[4,2,144,128]{3,2,1,0:T(8,128)(2,1)} %get-tuple-element.21), calls=%async_computation | async-start | bytes 589824 | tf_op jit(solution)/shard_map/all_to_all | solution.py:482
  8.1 0.0 copy-start.6
  8.1 10.5 %collective-permute-start.1 = (bf16[2,6,6,13,128]{4,3,2,1,0:T(8,128)(2,1)S(1)}, bf16[2,6,6,13,128]{4,3,2,1,0:T(8,128)(2,1)S(1)}, u32[]{:S(2)}, u32[]{:S(2)}) collective-permute-start(bf16[2,6,6,13,128]{4,3,2,1,0:T(8,128)(2,1)S(1)} %get-tuple-element.20), channel_id=1, source_target_pairs={{0,8},{16,24},{32,40},{48,56},{64,72},{80,88},{96,104},{112,120},{... | collective-permute-start | bytes 718856 | tf_op jit(solution)/shard_map/ppermute | solution.py:443
  18.6 1.9 %collective-permute-start = (bf16[2,6,6,13,128]{4,3,2,1,0:T(8,128)(2,1)S(1)}, bf16[2,6,6,13,128]{4,3,2,1,0:T(8,128)(2,1)S(1)}, u32[]{:S(2)}, u32[]{:S(2)}) collective-permute-start(bf16[2,6,6,13,128]{4,3,2,1,0:T(8,128)(2,1)S(1)} %get-tuple-element.19), channel_id=1, source_target_pairs={{8,16},{24,32},{40,48},{56,64},{72,80},{88,96},{104,112},{120,128}... | collective-permute-start | bytes 718856 | tf_op jit(solution)/shard_map/ppermute | solution.py:443
  20.5 0.0 copy-done
  20.5 0.0 copy-done.1
  20.5 0.0 copy-done.6
  20.5 3.8 %shard_map.86 = (bf16[6,6,6,13,128]{4,3,2,1,0:T(8,128)(2,1)}, bf16[6,6,6,13,128]{4,3,2,1,0:T(8,128)(2,1)}, bf16[2,2,6,6,13,128]{5,4,3,2,1,0:T(8,128)(2,1)}, bf16...) custom-call(bf16[6,6,6,13,128]{4,3,2,1,0:T(8,128)(2,1)S(1)} %bitcast.24, ...), custom_call_target="tpu_custom_call" | custom-call | flops 2147483648 | bytes 8388608 | tf_op jit(solution)/shard_map/pallas_call | solution.py:486
  24.4 0.0 collective-permute-done.1.first_ref
  24.4 0.0 all-to-all-done.bottom_ref
  24.4 0.9 %shard_map.87 = (bf16[2,16,128]{2,1,0:T(8,128)(2,1)S(1)}, f32[13,128]{1,0:T(8,128)S(1)}, s32[1,128]{1,0:T(1,128)S(1)}, s32[1,128]{1,0:T(1,128)S(1)}) custom-call(bf16[2,6,6,13,128]{4,3,2,1,0:T(8,128)(2,1)S(1)} %collective-permute-done.1.first_ref, bf16[4,2,144,128]{3,2,1,0:T(8,128)(2,1)S(1)} %all-to-all-done.bottom_ref, ...), custom_call_target="tpu_custom_call" | custom-call | flops 536870912 | bytes 4194304 | tf_op jit(solution)/shard_map/pallas_call | solution.py:519
  25.3 1.3 %collective-permute-done.second_ref = bf16[2,6,6,13,128]{4,3,2,1,0:T(8,128)(2,1)S(1)} collective-permute-done((bf16[2,6,6,13,128]{4,3,2,1,0:T(8,128)(2,1)S(1)}, bf16[2,6,6,13,128]{4,3,2,1,0:T(8,128)(2,1)S(1)}, u32[]{:S(2)}, u32[]{:S(2)}) %collective-permute-start) | collective-permute-done | bytes 239648 | tf_op jit(solution)/shard_map/ppermute | solution.py:443
  26.6 0.0 copy-start.2
  26.6 0.0 copy-start.3
  26.6 0.0 copy-start.5
  26.6 0.3 shard_map.88
  26.9 0.0 copy-start.4
  26.9 11.8 %all_to_all.10.got_ref = bf16[8,48,128]{2,1,0:T(8,128)(2,1)S(1)} all-to-all(bf16[8,48,128]{2,1,0:T(8,128)(2,1)S(1)} %shard_map.88), channel_id=1, replica_groups=mesh['layer'=4,'gx'=24,'gy'=8] {'gy'}, dimensions={0} | all-to-all | bytes 196608 | tf_op jit(solution)/shard_map/all_to_all | solution.py:548
  38.8 0.0 copy-done.2
  38.8 0.0 copy-done.3
  38.8 0.0 copy-done.5
  38.8 0.0 copy-done.4
  38.8 1.6 %shard_map.89 = (bf16[6,6,6,13,128]{4,3,2,1,0:T(8,128)(2,1)}, bf16[6,6,6,13,128]{4,3,2,1,0:T(8,128)(2,1)}, f32[13,1,128]{2,1,0:T(1,128)}) custom-call(bf16[8,48,128]{2,1,0:T(8,128)(2,1)S(1)} %all_to_all.10.got_ref, f32[8,16,128]{2,1,0:T(8,128)S(1)} %copy-done.5, ...), custom_call_target="tpu_custom_call", output_to_operand_aliasing={{0}: (11, {}), {1}: (12, {})} | custom-call | tf_op jit(solution)/shard_map/pallas_call | solution.py:550
Async XLA Ops:
  0.6 19.9 %copy-start = (bf16[13,1,1,6,6,6,128]{6,0,5,4,3,2,1:T(8,128)(2,1)S(1)}, bf16[13,1,1,6,6,6,128]{6,0,5,4,3,2,1:T(8,128)(2,1)}, u32[]{:S(2)}) copy-start(bf16[13,1,1,6,6,6,128]{6,0,5,4,3,2,1:T(8,128)(2,1)} %param.7) | copy-start | bytes 2156548
  0.6 19.9 %copy-start.1 = (bf16[13,1,1,6,6,6,128]{6,0,5,4,3,2,1:T(8,128)(2,1)S(1)}, bf16[13,1,1,6,6,6,128]{6,0,5,4,3,2,1:T(8,128)(2,1)}, u32[]{:S(2)}) copy-start(bf16[13,1,1,6,6,6,128]{6,0,5,4,3,2,1:T(8,128)(2,1)} %param.6) | copy-start | bytes 2156548
  2.7 21.7 %all-to-all-start = ((bf16[4,2,144,128]{3,2,1,0:T(8,128)(2,1)}), bf16[4,2,144,128]{3,2,1,0:T(8,128)(2,1)S(1)}, u32[]{:S(2)}, u32[]{:S(2)}) async-start(bf16[4,2,144,128]{3,2,1,0:T(8,128)(2,1)} %get-tuple-element.21), calls=%async_computation | async-start | bytes 589824 | tf_op jit(solution)/shard_map/all_to_all | solution.py:482
  8.1 12.4 %copy-start.6 = (f32[13,1,1,128]{3,2,1,0:T(1,128)S(1)}, f32[13,1,1,128]{3,2,1,0:T(1,128)}, u32[]{:S(2)}) copy-start(f32[13,1,1,128]{3,2,1,0:T(1,128)} %param.9) | copy-start | bytes 19972
  8.1 16.3 %collective-permute-start.1 = (bf16[2,6,6,13,128]{4,3,2,1,0:T(8,128)(2,1)S(1)}, bf16[2,6,6,13,128]{4,3,2,1,0:T(8,128)(2,1)S(1)}, u32[]{:S(2)}, u32[]{:S(2)}) collective-permute-start(bf16[2,6,6,13,128]{4,3,2,1,0:T(8,128)(2,1)S(1)} %get-tuple-element.20), channel_id=1, source_target_pairs={{0,8},{16,24},{32,40},{48,56},{64,72},{80,88},{96,104},{112,120},{... | collective-permute-start | bytes 718856 | tf_op jit(solution)/shard_map/ppermute | solution.py:443
  18.6 8.0 %collective-permute-start = (bf16[2,6,6,13,128]{4,3,2,1,0:T(8,128)(2,1)S(1)}, bf16[2,6,6,13,128]{4,3,2,1,0:T(8,128)(2,1)S(1)}, u32[]{:S(2)}, u32[]{:S(2)}) collective-permute-start(bf16[2,6,6,13,128]{4,3,2,1,0:T(8,128)(2,1)S(1)} %get-tuple-element.19), channel_id=1, source_target_pairs={{8,16},{24,32},{40,48},{56,64},{72,80},{88,96},{104,112},{120,128}... | collective-permute-start | bytes 718856 | tf_op jit(solution)/shard_map/ppermute | solution.py:443
  26.6 12.1 %copy-start.2 = (bf16[2,2,6,6,13,128]{5,4,3,2,1,0:T(8,128)(2,1)S(1)}, bf16[2,2,6,6,13,128]{5,4,3,2,1,0:T(8,128)(2,1)}, u32[]{:S(2)}) copy-start(bf16[2,2,6,6,13,128]{5,4,3,2,1,0:T(8,128)(2,1)} %get-tuple-element.27.side_ref) | copy-start | bytes 1437700
  26.6 12.1 %copy-start.3 = (bf16[2,4,2,5,13,128]{5,4,3,2,1,0:T(8,128)(2,1)S(1)}, bf16[2,4,2,5,13,128]{5,4,3,2,1,0:T(8,128)(2,1)}, u32[]{:S(2)}) copy-start(bf16[2,4,2,5,13,128]{5,4,3,2,1,0:T(8,128)(2,1)} %get-tuple-element.26.strip_ref) | copy-start | bytes 798724
  26.6 12.1 %copy-start.5 = (f32[8,16,128]{2,1,0:T(8,128)S(1)}, f32[8,16,128]{2,1,0:T(8,128)}, u32[]{:S(2)}) copy-start(f32[8,16,128]{2,1,0:T(8,128)} %get-tuple-element.22.small_hbm.small) | copy-start | bytes 196612
  26.9 11.9 %copy-start.4 = (bf16[2,4,6,13,128]{4,3,2,1,0:T(8,128)(2,1)S(1)}, bf16[2,4,6,13,128]{4,3,2,1,0:T(8,128)(2,1)}, u32[]{:S(2)}) copy-start(bf16[2,4,6,13,128]{4,3,2,1,0:T(8,128)(2,1)} %get-tuple-element.28.top_ref) | copy-start | bytes 479236
